TPU v7x, 32 devices: a whole 2x2x4 slice. The times are simulated.
32 devices in a mesh: lon: 16 (over z, y, core), lat: 2 (over x).
Axes of the slice: x: 2, y: 2, z: 4, core: 2. Of those that a mesh axis runs over, the one named last changes fastest.
Arguments:
- pressure: float32 [128, 256, 256], P(None, 'lon', 'lat'), may hold values from -10 to 10
- ocean_mask: int32 [256, 256], P('lon', 'lat'), may hold values 0 or 1
Outputs:
- modes: float32 [128, 3, 256, 256], P(None, None, 'lon', 'lat')
- factor_r: float32 [128, 128], replicated
All inputs are finite; a program needn't handle non-finite values. No bound on the sum of `ocean_mask` on one device may be relied on, other than what follows from the above.
Results may differ from a plain program's by a relative error of at most 0.0003.
Values sent between devices are 32-bit elements; how exact they have to be, the bound alone decides.
No kernel may reach another device: no remote copies, remote signals or barrier semaphores. Data moves between devices by JAX's collectives and lax.ppermute only.
A program may use at most 64 MiB of HBM per device.

v0:
```python
import functools

import jax
import jax.numpy as jnp
from jax import lax
from jax.experimental import pallas as pl
from jax.experimental.pallas import tpu as pltpu
from jax.sharding import PartitionSpec as P

PASSES = 4
HALO = PASSES + 1
EDGE = 8
ROUND = 1.5 * 2.0**23
BOTH = ("lon", "lat")
HIGHEST = lax.Precision.HIGHEST
VMEM = pl.BlockSpec(memory_space=pltpu.VMEM)
ANYWHERE = pl.BlockSpec(memory_space=pl.ANY)
PARAMS = pltpu.CompilerParams(vmem_limit_bytes=24 * 2**20)
SMALL = pltpu.CompilerParams(vmem_limit_bytes=12 * 2**20)


def place():
    lat = lax.axis_index("lat")
    return 1 - lax.rem(lax.axis_index("lon"), 2), lat, lat > 0, lat < lax.axis_size("lat") - 1


def f32(*shape):
    return jax.ShapeDtypeStruct(shape, jnp.float32)


def power_of_two(value):
    scaled = value * (2.0**23 + 1.0)
    return scaled - (scaled - value)


def dot_nt(left, right):
    return lax.dot_general(
        left, right, (((1,), (1,)), ((), ())), preferred_element_type=jnp.float32
    )


def dot_nn(left, right, precision=None):
    return lax.dot_general(
        left,
        right,
        (((1,), (0,)), ((), ())),
        precision=precision,
        preferred_element_type=jnp.float32,
    )


def slices_of(scaled):
    first = (scaled + ROUND) - ROUND
    rest = (scaled - first) * 256.0
    second = (rest + ROUND) - ROUND
    rest = (rest - second) * 256.0
    third = (rest + ROUND) - ROUND
    return first, second, third


def longitude(backwards, row, clon):
    return row + backwards * (clon - 1 - 2 * row)


def prepare_kernel(pressure_ref, mask_ref, turned_ref, mask_out_ref, *edge_refs, clon, clat, snaps):
    backwards, lat, _, _ = place()
    line = lax.broadcasted_iota(jnp.int32, (EDGE, clat), 0)
    for row in range(clon):
        spot = longitude(backwards, row, clon)
        plane = pressure_ref[pl.ds(spot, snaps, stride=clon), :].T
        mask = mask_ref[pl.ds(spot, 1), :].astype(jnp.float32)
        turned_ref[row] = plane
        mask_out_ref[row : row + 1] = mask
        low = jnp.where(line < HALO, plane[:EDGE], mask)
        high = jnp.where(line >= EDGE - HALO, plane[clat - EDGE :], mask)
        ends = (low, high) if len(edge_refs) == 2 else (jnp.where(lat == 0, high, low),)
        for edge_ref, end in zip(edge_refs, ends):
            edge_ref[row] = end


def prepare(pressure, mask, edges):
    snaps, clon, clat = pressure.shape
    body = functools.partial(prepare_kernel, clon=clon, clat=clat, snaps=snaps)
    return pl.pallas_call(
        body,
        out_shape=[f32(clon, clat, snaps), f32(clon, clat)]
        + [f32(clon, EDGE, snaps)] * edges,
        in_specs=[VMEM, VMEM],
        compiler_params=SMALL,
        name="prepare",
    )(pressure.reshape(snaps * clon, clat), mask)


def ends_of(left_ref, right_ref, row, has_left, has_right):
    left, right = left_ref[row], right_ref[row]
    return (
        jnp.where(has_left, left, 0.0),
        jnp.where(has_right, right, 0.0),
        jnp.where(has_left, left[:1], 0.0),
        jnp.where(has_right, right[EDGE - 1 :], 0.0),
    )


def pack_kernel(turned_ref, mask_ref, left_ref, right_ref, near_ref, far_ref, *, clon, clat):
    _, _, has_left, has_right = place()
    zeros = jnp.zeros((EDGE - 3, clat), jnp.float32)
    for which, out_ref in enumerate((near_ref, far_ref)):
        for i in range(HALO):
            row = clon - 1 - i if which else i
            left, right, left_mask, right_mask = ends_of(left_ref, right_ref, row, has_left, has_right)
            out_ref[i, :EDGE] = left
            out_ref[i, EDGE : EDGE + clat] = turned_ref[row]
            out_ref[i, EDGE + clat : 2 * EDGE + clat] = right
            out_ref[i, 2 * EDGE + clat :] = jnp.concatenate(
                [mask_ref[row : row + 1], left_mask, right_mask, zeros], axis=0
            )


def pack(turned, mask, left, right):
    clon, clat, snaps = turned.shape
    block = f32(HALO, clat + 3 * EDGE, snaps)
    return pl.pallas_call(
        functools.partial(pack_kernel, clon=clon, clat=clat),
        out_shape=[block, block],
        in_specs=[VMEM] * 4,
        compiler_params=SMALL,
        name="pack",
    )(turned, mask, left, right)


class Tables:
    def __init__(self, masks, keep_lon, keep_lat, quarter):
        self.masks = masks
        self.keep_lon = keep_lon
        self.keep_lat = keep_lat
        self.quarter = quarter

    def put_masks(self, row, own, left, right):
        for which, value in enumerate((own, left, right)):
            self.masks[which, row : row + 1] = value

    def fill(self, rows, clat):
        padded = self.masks.shape[1]
        own, left, right = self.masks[0], self.masks[1], self.masks[2]
        lane = lax.broadcasted_iota(jnp.int32, (padded, clat), 1)
        first_lane = lane == 0
        last_lane = lane == clat - 1

        def up(mask):
            return pltpu.roll(mask, 1, 1)

        def down(mask):
            return pltpu.roll(mask, clat - 1, 1)

        def coefficients(mask, south, north):
            across = pltpu.roll(mask, 1, 0) + pltpu.roll(mask, padded - 1, 0)
            return (
                mask * (1.0 - 0.25 * across),
                mask * (1.0 - 0.25 * (south + north)),
                0.25 * mask,
            )

        middle = coefficients(
            own,
            jnp.where(first_lane, up(left), up(own)),
            jnp.where(last_lane, down(right), down(own)),
        )
        lower = coefficients(left, up(left), jnp.where(last_lane, down(own), down(left)))
        upper = coefficients(right, jnp.where(first_lane, up(own), up(right)), down(right))
        for which, table in enumerate((self.keep_lon, self.keep_lat, self.quarter)):
            column = jnp.concatenate(
                [lower[which].T[clat - EDGE :], middle[which].T, upper[which].T[:EDGE]], axis=0
            )
            for row in rows:
                table[row] = jnp.broadcast_to(
                    column[:, row : row + 1], (clat + 2 * EDGE, table.shape[2])
                )


def sweep(tables, source, target, swept, begin, end, tall):
    lower, upper = EDGE, EDGE + tall

    def one(row, carry):
        around = source[row - 1, lower:upper] + source[row + 1, lower:upper]
        near = tables.quarter[row]
        middle = tables.keep_lon[row] * source[row, lower:upper] + near * around
        swept[row, lower:upper] = middle
        around = swept[row, lower - 1 : upper - 1] + swept[row, lower + 1 : upper + 1]
        target[row, lower:upper] = tables.keep_lat[row] * middle + near * around
        return carry

    lax.fori_loop(begin, end, one, 0)


def clear_ends(swept, rows, tall, snaps):
    zeros = jnp.zeros((EDGE, snaps), jnp.float32)
    for row in rows:
        swept[row, :EDGE] = zeros
        swept[row, EDGE + tall :] = zeros


def fields_of(backwards, tables, source, planes, x_ref, sems, rows, offset, clon, clat, snaps):
    begin = 2 * EDGE
    end = begin + clat
    count = len(rows)
    sign = jnp.where(backwards > 0, -2.0, 2.0)

    def copy(which, i):
        spot = which * count + i
        to = which * clon + longitude(backwards, rows[0] + i, clon)
        return pltpu.make_async_copy(planes.at[spot], x_ref.at[to], sems.at[spot])

    def one(i, top):
        here = rows[0] + i + offset
        center = source[here, begin:end]
        quarter = tables.quarter[here, EDGE : EDGE + clat]
        along_lon = (quarter * sign) * (source[here + 1, begin:end] - source[here - 1, begin:end])
        along_lat = (quarter * 2.0) * (
            source[here, begin + 1 : end + 1] - source[here, begin - 1 : end - 1]
        )
        for which, value in enumerate((center, along_lon, along_lat)):
            value = value.T
            planes[which * count + i] = value
            top = jnp.maximum(top, jnp.abs(value))
        for which in range(3):
            copy(which, i).start()
        return top

    top = lax.fori_loop(0, count, one, jnp.zeros((snaps, clat), jnp.float32))

    def finish():
        def wait(i, carry):
            for which in range(3):
                copy(which, i).wait()
            return carry

        lax.fori_loop(0, count, wait, 0)

    return top, finish


def gram_of(planes, count, top, snaps, clat):
    unit = power_of_two(jnp.maximum(jnp.max(top, axis=1, keepdims=True), 2.0**-60))
    to_whole = jnp.broadcast_to(128.0 / unit, (snaps, clat))
    whole = jnp.zeros((snaps, snaps), jnp.int32)
    first_second = jnp.zeros((snaps, snaps), jnp.float32)
    second_any = jnp.zeros((snaps, 2 * snaps), jnp.float32)
    third_any = jnp.zeros((snaps, 2 * snaps), jnp.float32)
    for begin in range(0, count, 2):
        parts = [slices_of(planes[which] * to_whole) for which in range(begin, min(begin + 2, count))]
        a, b, c = [
            jnp.concatenate([piece.astype(jnp.bfloat16) for piece in same], axis=1) for same in zip(*parts)
        ]
        from_first = dot_nt(a, jnp.concatenate([a, b], axis=0))
        whole = whole + from_first[:, :snaps].astype(jnp.int32)
        first_second = first_second + from_first[:, snaps:]
        second_any = second_any + dot_nt(b, jnp.concatenate([b, c], axis=0))
        third_any = third_any + dot_nt(c, jnp.concatenate([a, c], axis=0))
    fine = (
        first_second
        + (second_any[:, :snaps] * 2.0**-9 + second_any[:, snaps:] * 2.0**-16)
        + (third_any[:, :snaps] * 2.0**-8 + third_any[:, snaps:] * 2.0**-25)
    )
    head = whole.astype(jnp.float32)
    tail = (whole - head.astype(jnp.int32)).astype(jnp.float32) + (fine + fine.T) * 2.0**-8
    total = head + tail
    tail = tail - (total - head)
    unit = jnp.broadcast_to(unit * (1.0 / 128.0), (snaps, snaps))
    return total * unit * unit.T, tail * unit * unit.T


def add_pairs(left, right):
    total = left[0] + right[0]
    moved = total - left[0]
    lost = (left[0] - (total - moved)) + (right[0] - moved)
    return total, lost + (left[1] + right[1])


def put_gram(gram_ref, head, tail):
    half = head.shape[0] // 2
    for core in range(2):
        gram_ref[core, 0] = head[core * half : (core + 1) * half]
        gram_ref[core, 1] = tail[core * half : (core + 1) * half]


def near_kernel(
    turned_ref, mask_ref, left_ref, right_ref, near_ref, x_ref, rim_ref, gram_ref,
    field_a, field_b, swept, masks, keep_lon, keep_lat, quarter, planes, sems, *, clon, clat, snaps,
):
    tall = clat + 2 * EDGE
    lower, upper = EDGE, EDGE + tall
    tables = Tables(masks, keep_lon, keep_lat, quarter)
    wide = clon + HALO
    backwards, _, has_left, has_right = place()
    for i in range(HALO):
        marks = near_ref[i, tall:]
        tables.put_masks(HALO - 1 - i, marks[0:1], marks[1:2], marks[2:3])
    for row in range(clon):
        ends = ends_of(left_ref, right_ref, row, has_left, has_right)
        tables.put_masks(HALO + row, mask_ref[row : row + 1], *ends[2:])
    for row in range(wide, masks.shape[1]):
        zero = jnp.zeros((1, clat), jnp.float32)
        tables.put_masks(row, zero, zero, zero)
    tables.fill(range(wide), clat)
    clear_ends(swept, range(wide), tall, snaps)
    for i in range(HALO):
        row = HALO - 1 - i
        field_a[row, lower:upper] = near_ref[i, :tall] * (quarter[row] * 4.0)

    def start_row(row, carry):
        here = row + HALO
        kept = quarter[here] * 4.0
        left, right, _, _ = ends_of(left_ref, right_ref, row, has_left, has_right)
        field_a[here, lower : lower + EDGE] = left * kept[:EDGE]
        field_a[here, lower + EDGE : upper - EDGE] = turned_ref[row] * kept[EDGE : EDGE + clat]
        field_a[here, upper - EDGE : upper] = right * kept[EDGE + clat :]
        return carry

    lax.fori_loop(0, clon, start_row, 0)
    source, target = field_a, field_b
    for step in range(PASSES + 1):
        rim_ref[step] = source[wide - 2 - step : wide - step, lower:upper]
        if step < PASSES:
            sweep(tables, source, target, swept, step + 1, wide - 1 - step, tall)
            source, target = target, source
    rows = range(clon - HALO)
    top, finish = fields_of(backwards, tables, source, planes, x_ref, sems, rows, HALO, clon, clat, snaps)
    put_gram(gram_ref, *gram_of(planes, 3 * len(rows), top, snaps, clat))
    finish()


def far_kernel(
    mask_ref, left_ref, right_ref, far_ref, rim_ref, gram_in_ref, x_in_ref, x_ref, gram_ref,
    field_a, field_b, swept, masks, keep_lon, keep_lat, quarter, planes, sems, *, clon, clat, snaps,
):
    tall = clat + 2 * EDGE
    lower, upper = EDGE, EDGE + tall
    tables = Tables(masks, keep_lon, keep_lat, quarter)
    backwards, _, has_left, has_right = place()
    skip = clon - HALO - 1
    wide = 2 * HALO + 1
    for row in range(skip, clon):
        ends = ends_of(left_ref, right_ref, row, has_left, has_right)
        tables.put_masks(row - skip, mask_ref[row : row + 1], *ends[2:])
    for i in range(HALO):
        marks = far_ref[i, tall:]
        tables.put_masks(HALO + 1 + i, marks[0:1], marks[1:2], marks[2:3])
    for row in range(wide, masks.shape[1]):
        zero = jnp.zeros((1, clat), jnp.float32)
        tables.put_masks(row, zero, zero, zero)
    tables.fill(range(1, wide), clat)
    clear_ends(swept, range(1, wide - 1), tall, snaps)
    for i in range(HALO):
        row = HALO + 1 + i
        field_a[row, lower:upper] = far_ref[i, :tall] * (quarter[row] * 4.0)
    source, target = field_a, field_b
    for step in range(PASSES + 1):
        source[HALO - 1 - step : HALO + 1 - step, lower:upper] = rim_ref[step]
        if step < PASSES:
            sweep(tables, source, target, swept, HALO - step, 2 * HALO - step, tall)
            source, target = target, source
    rows = range(clon - HALO, clon)
    top, finish = fields_of(backwards, tables, source, planes, x_ref, sems, rows, -skip, clon, clat, snaps)
    gram = gram_of(planes, 3 * len(rows), top, snaps, clat)
    before = [jnp.concatenate([gram_in_ref[0, part], gram_in_ref[1, part]], axis=0) for part in range(2)]
    put_gram(gram_ref, *add_pairs(before, gram))
    finish()


def filter_scratch(wide, planes, clat, snaps):
    tall = clat + 2 * EDGE
    field = pltpu.VMEM((wide, tall + 2 * EDGE, snaps), jnp.float32)
    table = pltpu.VMEM((wide, tall, snaps), jnp.float32)
    masks = pltpu.VMEM((3, -(-wide // 8) * 8, clat), jnp.float32)
    return [
        field, field, field, masks, table, table, table,
        pltpu.VMEM((planes, snaps, clat), jnp.float32),
        pltpu.SemaphoreType.DMA((planes,)),
    ]


def near_part(turned, mask, left, right, near):
    clon, clat, snaps = turned.shape
    planes = 3 * (clon - HALO)
    return pl.pallas_call(
        functools.partial(near_kernel, clon=clon, clat=clat, snaps=snaps),
        out_shape=[
            f32(3 * clon, snaps, clat),
            f32(PASSES + 1, 2, clat + 2 * EDGE, snaps),
            f32(2, 2, snaps // 2, snaps),
        ],
        in_specs=[VMEM] * 5,
        out_specs=[ANYWHERE, VMEM, VMEM],
        scratch_shapes=filter_scratch(clon + HALO, planes, clat, snaps),
        compiler_params=PARAMS,
        cost_estimate=pl.CostEstimate(flops=4_000_000_000, bytes_accessed=8_000_000, transcendentals=0),
        name="near_part",
    )(turned, mask, left, right, near)


def far_part(mask, left, right, far, rim, gram, x, clon, clat, snaps):
    planes = 3 * HALO
    return pl.pallas_call(
        functools.partial(far_kernel, clon=clon, clat=clat, snaps=snaps),
        out_shape=[f32(3 * clon, snaps, clat), f32(2, 2, snaps // 2, snaps)],
        in_specs=[VMEM] * 6 + [ANYWHERE],
        out_specs=[ANYWHERE, VMEM],
        scratch_shapes=filter_scratch(2 * HALO + 1, planes, clat, snaps),
        input_output_aliases={6: 0},
        compiler_params=PARAMS,
        name="far_part",
    )(mask, left, right, far, rim, gram, x)


def spread(row, lane):
    return jnp.broadcast_to(row[:, lane : lane + 1], row.shape)


def eliminate(matrix):
    size = matrix.shape[0]
    count = size // 8
    tiles = [matrix[8 * i : 8 * i + 8, :] for i in range(count)]
    lane = lax.broadcasted_iota(jnp.int32, (8, size), 1)
    sub = lax.broadcasted_iota(jnp.int32, (8, size), 0)
    uppers, inverses = [], []
    for block in range(count):
        base = 8 * block
        panel = tiles[block]
        inside = (lane >= base) & (lane < base + 8)
        rows = [jnp.broadcast_to(panel[r : r + 1, :], (8, size)) for r in range(8)]
        entry = {(r, c): spread(rows[r], base + c) for r in range(8) for c in range(r + 1)}
        units = [jnp.where(lane == base + r, 1.0, 0.0) for r in range(8)]
        factor = {}
        pivots = []
        for k in range(8):
            pivots.append(1.0 / entry[k, k])
            for r in range(k + 1, 8):
                factor[r, k] = entry[r, k] * pivots[k]
            for r in range(k + 1, 8):
                for c in range(k + 1, r + 1):
                    entry[r, c] = entry[r, c] - factor[r, k] * entry[c, k]
        for k in range(8):
            for r in range(k + 1, 8):
                rows[r] = rows[r] - factor[r, k] * rows[k]
                units[r] = units[r] - factor[r, k] * units[k]
        joined = [jnp.where(inside, units[r], rows[r]) for r in range(8)]
        for i in range(block + 1, count):
            raw = [spread(tiles[i], base + k) for k in range(8)]
            tile = jnp.where(inside, 0.0, tiles[i])
            for k in range(8):
                scaled = raw[k] * pivots[k]
                for q in range(k + 1, 8):
                    raw[q] = raw[q] - scaled * entry[q, k]
                tile = tile - scaled * joined[k]
            tiles[i] = tile
        upper = jnp.zeros((8, size), jnp.float32)
        inverse = jnp.zeros((8, size), jnp.float32)
        for r in range(8):
            scale = lax.rsqrt(entry[r, r])
            upper = jnp.where(sub == r, rows[r] * scale, upper)
            inverse = jnp.where(sub == r, joined[r] * scale, inverse)
        uppers.append(jnp.where(lane >= base + sub, upper, 0.0))
        inverses.append(jnp.where(lane <= base + sub, inverse, 0.0))
    return jnp.concatenate(uppers, axis=0), jnp.concatenate(inverses, axis=0)


def thirds(value):
    first = value.astype(jnp.bfloat16)
    rest = value - first.astype(jnp.float32)
    second = rest.astype(jnp.bfloat16)
    third = (rest - second.astype(jnp.float32)).astype(jnp.bfloat16)
    return first, second, third


def modes_kernel(gram_ref, x_ref, modes_ref, factor_ref, x_vmem, out_vmem, in_sem, out_sems, *, clon, clat, snaps, total_rows):
    load = pltpu.make_async_copy(x_ref, x_vmem, in_sem)
    load.start()
    head, tail = [jnp.concatenate([gram_ref[0, part], gram_ref[1, part]], axis=0) for part in range(2)]
    row = lax.broadcasted_iota(jnp.int32, (snaps, snaps), 0)
    col = lax.broadcasted_iota(jnp.int32, (snaps, snaps), 1)
    diagonal = jnp.where(row == col, head, 0.0)
    grow = power_of_two(jnp.sqrt(jnp.sum(diagonal, axis=1, keepdims=True)))
    shrink_rows = jnp.broadcast_to(1.0 / grow, (snaps, snaps))
    shrink_cols = shrink_rows.T
    head = head * shrink_rows * shrink_cols
    tail = tail * shrink_rows * shrink_cols

    upper_one, inverse_one = eliminate(head)

    first, second, third = slices_of(upper_one.T * 128.0)
    a = first.astype(jnp.bfloat16)
    b = second.astype(jnp.bfloat16)
    c = third.astype(jnp.bfloat16)
    exact = dot_nt(a, a)
    mixed = dot_nt(a, b)
    mixed_small = (
        dot_nt(a, c) + dot_nt(b, b) * 0.5 + dot_nt(b, c) * 2.0**-8 + dot_nt(c, c) * 2.0**-17
    )
    mixed = mixed + mixed.T
    mixed_small = mixed_small + mixed_small.T
    missing = (head - exact * 2.0**-14) - mixed * 2.0**-22
    missing = missing - mixed_small * 2.0**-30 + tail
    lower_one = (first + second * 2.0**-8 + third * 2.0**-16) * (1.0 / 128.0)

    near_one = dot_nn(inverse_one, lower_one, HIGHEST)
    left_over = dot_nn(dot_nn(inverse_one, missing, HIGHEST), inverse_one.T, HIGHEST)
    gram_two = dot_nn(near_one, near_one.T, HIGHEST) + left_over
    gram_two = 0.5 * (gram_two + gram_two.T)
    upper_two, inverse_two = eliminate(gram_two)

    scale = float(total_rows) ** 0.5
    combined = dot_nn(inverse_two, inverse_one, HIGHEST) * shrink_cols * scale
    first, second, third = thirds(combined)
    first_second = jnp.concatenate([first, second], axis=1)
    first_third = jnp.concatenate([first, third], axis=1)
    load.wait()
    copies = []
    for which in range(3):
        for part in range(clon // 8):
            spot = which * (clon // 8) + part
            flat = out_vmem.at[spot].reshape(snaps * 8, clat)
            for lon in range(0, 8, 2):
                plane = which * clon + part * 8 + lon
                x_one, x_two, x_three = thirds(jnp.concatenate([x_vmem[plane], x_vmem[plane + 1]], axis=1))
                value = (
                    dot_nn(first_third, jnp.concatenate([x_three, x_one], axis=0))
                    + dot_nn(first_second, jnp.concatenate([x_two, x_two], axis=0))
                ) + dot_nn(first_second, jnp.concatenate([x_one, x_one], axis=0))
                flat[pl.ds(lon, snaps, stride=8), :] = value[:, :clat]
                flat[pl.ds(lon + 1, snaps, stride=8), :] = value[:, clat:]
            copy = pltpu.make_async_copy(
                out_vmem.at[spot], modes_ref.at[:, which, pl.ds(part * 8, 8), :], out_sems.at[spot]
            )
            copy.start()
            copies.append(copy)
    factor = dot_nn(upper_two, lower_one.T, HIGHEST) * jnp.broadcast_to(grow, (snaps, snaps)).T
    factor_ref[...] = jnp.where(col >= row, factor * (1.0 / scale), 0.0)
    for copy in copies:
        copy.wait()


def orthonormal(gram, x, clon, clat, total_rows):
    snaps = gram.shape[3]
    parts = 3 * clon // 8
    return pl.pallas_call(
        functools.partial(modes_kernel, clon=clon, clat=clat, snaps=snaps, total_rows=total_rows),
        out_shape=[f32(snaps, 3, clon, clat), f32(snaps, snaps)],
        in_specs=[VMEM, ANYWHERE],
        out_specs=[ANYWHERE, VMEM],
        scratch_shapes=[
            pltpu.VMEM((3 * clon, snaps, clat), jnp.float32),
            pltpu.VMEM((parts, snaps, 8, clat), jnp.float32),
            pltpu.SemaphoreType.DMA,
            pltpu.SemaphoreType.DMA((parts,)),
        ],
        compiler_params=PARAMS,
        name="orthonormal",
    )(gram, x)


def summed(halves, nlon, nlat):
    count = nlon * nlat
    core = lax.axis_index("lon") % 2

    def partner(value, step):
        return lax.ppermute(value, BOTH, [(i, i ^ step) for i in range(count)])

    def add(left, right):
        return jnp.stack(add_pairs(left, right))

    mine = add(
        jnp.where(core == 0, halves[0], halves[1]),
        partner(jnp.where(core == 0, halves[1], halves[0]), nlat),
    )
    steps = [1 << bit for bit in range(count.bit_length() - 1) if 1 << bit != nlat]
    while steps:
        if len(steps) >= 2:
            low, high = steps[0], steps[1]
            others = [partner(mine, step) for step in (low, high, low ^ high)]
            mine = add(add(mine, others[0]), add(others[1], others[2]))
            steps = steps[2:]
        else:
            mine = add(mine, partner(mine, steps[0]))
            steps = steps[1:]
    other = partner(mine, nlat)
    return jnp.where(core == 0, jnp.stack([mine, other]), jnp.stack([other, mine]))


def on_device(pressure, ocean_mask):
    snaps, clon, clat = pressure.shape
    nlon, nlat = lax.axis_size("lon"), lax.axis_size("lat")
    merged = nlat == 2
    turned, mask, *edges = prepare(pressure, ocean_mask, 1 if merged else 2)
    if merged:
        left = right = lax.ppermute(edges[0], "lat", [(0, 1), (1, 0)])
    else:
        left = lax.ppermute(edges[1], "lat", [(i, i + 1) for i in range(nlat - 1)])
        right = lax.ppermute(edges[0], "lat", [(i + 1, i) for i in range(nlat - 1)])
    near, far = pack(turned, mask, left, right)
    far = lax.ppermute(
        far, "lon", [(i, (i + 1 if i % 2 else i - 1) % nlon) for i in range(nlon)]
    )
    near = lax.ppermute(near, "lon", [(i, i ^ 1) for i in range(nlon)])
    x, rim, gram = near_part(turned, mask, left, right, near)
    x, gram = far_part(mask, left, right, far, rim, gram, x, clon, clat, snaps)
    gram = summed(gram, nlon, nlat)
    return tuple(orthonormal(gram, x, clon, clat, 3 * clon * clat * nlon * nlat))


def solution(mesh):
    return jax.shard_map(
        on_device,
        mesh=mesh,
        in_specs=(P(None, "lon", "lat"), P("lon", "lat")),
        out_specs=(P(None, None, "lon", "lat"), P()),
        check_vma=False,
    )
```

profile of v0, /device:TPU:0, one launch (start us, length us, event | category | flops | bytes accessed | tf_op | source)
XLA Modules:
  0.0 62.6 jit_solution(9055767335241221045)
XLA Ops:
  0.6 1.2 %copy-done = f32[128,16,128]{2,1,0:T(8,128)S(1)} copy-done((f32[128,16,128]{2,1,0:T(8,128)S(1)}, f32[128,16,128]{2,1,0:T(8,128)}, u32[]{:S(2)}) %copy-start) | copy-done | bytes 1048600
  1.9 0.7 %copy-done.1 = s32[16,128]{1,0:T(8,128)S(1)} copy-done((s32[16,128]{1,0:T(8,128)S(1)}, s32[16,128]{1,0:T(8,128)}, u32[]{:S(2)}) %copy-start.1) | copy-done | bytes 8216
  2.6 0.4 prepare.1
  2.9 3.0 %collective-permute-start = (f32[16,8,128]{2,1,0:T(8,128)S(1)}, f32[16,8,128]{2,1,0:T(8,128)S(1)}, u32[]{:S(2)}, u32[]{:S(2)}) collective-permute-start(f32[16,8,128]{2,1,0:T(8,128)S(1)} %get-tuple-element.13), channel_id=1, source_target_pairs={{0,1},{1,0},{2,3},{3,2},{4,5},{5,4},{6,7},{7,6},{8,9},{9,8},{10,11... | collective-permute-start | bytes 196616 | tf_op jit(solution)/shard_map/ppermute | solution.py:595
  5.9 2.2 %collective-permute-done.left_ref.right_ref = f32[16,8,128]{2,1,0:T(8,128)S(1)} collective-permute-done((f32[16,8,128]{2,1,0:T(8,128)S(1)}, f32[16,8,128]{2,1,0:T(8,128)S(1)}, u32[]{:S(2)}, u32[]{:S(2)}) %collective-permute-start) | collective-permute-done | bytes 65568 | tf_op jit(solution)/shard_map/ppermute | solution.py:595
  8.2 0.1 pack.1
  8.2 0.1 collective-permute-start.2
  8.3 5.2 %collective-permute-start.1 = (f32[5,152,128]{2,1,0:T(8,128)S(1)}, f32[5,152,128]{2,1,0:T(8,128)S(1)}, u32[]{:S(2)}, u32[]{:S(2)}) collective-permute-start(f32[5,152,128]{2,1,0:T(8,128)S(1)} %get-tuple-element.15), channel_id=1, source_target_pairs={{0,30},{2,4},{4,2},{6,8},{8,6},{10,12},{12,10},{14,16},{16,14},{18... | collective-permute-start | bytes 1167368 | tf_op jit(solution)/shard_map/ppermute | solution.py:600
  13.5 11.5 %near_part.1 = (f32[48,128,128]{2,1,0:T(8,128)S(1)}, f32[5,2,144,128]{3,2,1,0:T(8,128)S(1)}, f32[2,2,64,128]{3,2,1,0:T(8,128)S(1)}) custom-call(f32[16,128,128]{2,1,0:T(8,128)S(1)} %get-tuple-element.14.turned_ref, f32[16,128]{1,0:T(8,128)S(1)} %get-tuple-element.12.mask_ref, f32[16,8,128]{2,1,0:T(8,128)S(1)} %collective-permute-done.left_ref.right_ref, ...), custom_call_target="tpu_custom_call" | custom-call | flops 4000000000 | bytes 8000000 | tf_op jit(solution)/shard_map/near_part/pallas_call | solution.py:385
  25.0 5.1 %far_part.1 = (f32[48,128,128]{2,1,0:T(8,128)S(1)}, f32[2,2,64,128]{3,2,1,0:T(8,128)S(1)}) custom-call(f32[16,128]{1,0:T(8,128)S(1)} %get-tuple-element.12.mask_ref, f32[16,8,128]{2,1,0:T(8,128)S(1)} %collective-permute-done.left_ref.right_ref, f32[16,8,128]{2,1,0:T(8,128)S(1)} %collective-permute-done.left_ref.right_ref, ...), custom_call_target="tpu_custom_call", output_to_operand_aliasing={{0}: (6, {})} | custom-call | tf_op jit(solution)/shard_map/far_part/pallas_call | solution.py:403
  30.2 0.1 collective-permute-start.3
  30.3 1.2 %collective-permute-done.3 = f32[2,64,128]{2,1,0:T(8,128)S(1)} collective-permute-done((f32[2,64,128]{2,1,0:T(8,128)S(1)}, f32[2,64,128]{2,1,0:T(8,128)S(1)}, u32[]{:S(2)}, u32[]{:S(2)}) %collective-permute-start.3) | collective-permute-done | bytes 65568 | tf_op jit(solution)/shard_map/ppermute | solution.py:566
  31.6 1.6 %collective-permute-start.4 = (f32[2,64,128]{2,1,0:T(8,128)S(1)}, f32[2,64,128]{2,1,0:T(8,128)S(1)}, u32[]{:S(2)}, u32[]{:S(2)}) collective-permute-start(f32[2,64,128]{2,1,0:T(8,128)S(1)} %pad_maximum_fusion), channel_id=1, source_target_pairs={{0,1},{1,0},{2,3},{3,2},{4,5},{5,4},{6,7},{7,6},{8,9},{9,8},{10,11... | collective-permute-start | bytes 196616 | tf_op jit(solution)/shard_map/ppermute | solution.py:566
  33.1 2.0 %collective-permute-start.6 = (f32[2,64,128]{2,1,0:T(8,128)S(1)}, f32[2,64,128]{2,1,0:T(8,128)S(1)}, u32[]{:S(2)}, u32[]{:S(2)}) collective-permute-start(f32[2,64,128]{2,1,0:T(8,128)S(1)} %pad_maximum_fusion), channel_id=1, source_target_pairs={{0,5},{1,4},{2,7},{3,6},{4,1},{5,0},{6,3},{7,2},{8,13},{9,12},{10,... | collective-permute-start | bytes 196616 | tf_op jit(solution)/shard_map/ppermute | solution.py:566
  35.1 0.8 %collective-permute-done.4 = f32[2,64,128]{2,1,0:T(8,128)S(1)} collective-permute-done((f32[2,64,128]{2,1,0:T(8,128)S(1)}, f32[2,64,128]{2,1,0:T(8,128)S(1)}, u32[]{:S(2)}, u32[]{:S(2)}) %collective-permute-start.4) | collective-permute-done | bytes 65568 | tf_op jit(solution)/shard_map/ppermute | solution.py:566
  35.9 2.7 %collective-permute-done.5 = f32[2,64,128]{2,1,0:T(8,128)S(1)} collective-permute-done((f32[2,64,128]{2,1,0:T(8,128)S(1)}, f32[2,64,128]{2,1,0:T(8,128)S(1)}, u32[]{:S(2)}, u32[]{:S(2)}) %collective-permute-start.5) | collective-permute-done | bytes 65568 | tf_op jit(solution)/shard_map/ppermute | solution.py:566
  38.7 0.1 collective-permute-start.7
  38.7 2.4 %collective-permute-start.8 = (f32[2,64,128]{2,1,0:T(8,128)S(1)}, f32[2,64,128]{2,1,0:T(8,128)S(1)}, u32[]{:S(2)}, u32[]{:S(2)}) collective-permute-start(f32[2,64,128]{2,1,0:T(8,128)S(1)} %pad_maximum_fusion.1), channel_id=1, source_target_pairs={{0,16},{1,17},{2,18},{3,19},{4,20},{5,21},{6,22},{7,23},{8,24},{9,... | collective-permute-start | bytes 196616 | tf_op jit(solution)/shard_map/ppermute | solution.py:566
  41.1 2.0 %collective-permute-start.9 = (f32[2,64,128]{2,1,0:T(8,128)S(1)}, f32[2,64,128]{2,1,0:T(8,128)S(1)}, u32[]{:S(2)}, u32[]{:S(2)}) collective-permute-start(f32[2,64,128]{2,1,0:T(8,128)S(1)} %pad_maximum_fusion.1), channel_id=1, source_target_pairs={{0,24},{1,25},{2,26},{3,27},{4,28},{5,29},{6,30},{7,31},{8,16},{9,... | collective-permute-start | bytes 196616 | tf_op jit(solution)/shard_map/ppermute | solution.py:566
  43.1 1.6 %collective-permute-done.8 = f32[2,64,128]{2,1,0:T(8,128)S(1)} collective-permute-done((f32[2,64,128]{2,1,0:T(8,128)S(1)}, f32[2,64,128]{2,1,0:T(8,128)S(1)}, u32[]{:S(2)}, u32[]{:S(2)}) %collective-permute-start.8) | collective-permute-done | bytes 65568 | tf_op jit(solution)/shard_map/ppermute | solution.py:566
  44.7 2.5 %collective-permute-done.9 = f32[2,64,128]{2,1,0:T(8,128)S(1)} collective-permute-done((f32[2,64,128]{2,1,0:T(8,128)S(1)}, f32[2,64,128]{2,1,0:T(8,128)S(1)}, u32[]{:S(2)}, u32[]{:S(2)}) %collective-permute-start.9) | collective-permute-done | bytes 65568 | tf_op jit(solution)/shard_map/ppermute | solution.py:566
  47.2 0.1 collective-permute-start.10
  47.3 1.2 %collective-permute-done.10 = f32[2,64,128]{2,1,0:T(8,128)S(1)} collective-permute-done((f32[2,64,128]{2,1,0:T(8,128)S(1)}, f32[2,64,128]{2,1,0:T(8,128)S(1)}, u32[]{:S(2)}, u32[]{:S(2)}) %collective-permute-start.10) | collective-permute-done | bytes 65568 | tf_op jit(solution)/shard_map/ppermute | solution.py:566
  48.6 13.8 %orthonormal.1 = (f32[128,3,16,128]{3,2,1,0:T(8,128)}, f32[128,128]{1,0:T(8,128)}) custom-call(f32[2,2,64,128]{3,2,1,0:T(8,128)S(1)} %maximum_select_fusion.gram_ref, f32[48,128,128]{2,1,0:T(8,128)S(1)} %get-tuple-element.21.x_ref), custom_call_target="tpu_custom_call" | custom-call | tf_op jit(solution)/shard_map/orthonormal/pallas_call | solution.py:545
  (15 shorter events, 0.1 us)
Async XLA Ops:
  0.6 1.2 %copy-start = (f32[128,16,128]{2,1,0:T(8,128)S(1)}, f32[128,16,128]{2,1,0:T(8,128)}, u32[]{:S(2)}) copy-start(f32[128,16,128]{2,1,0:T(8,128)} %param.2) | copy-start | bytes 3145732
  1.9 0.7 %copy-start.1 = (s32[16,128]{1,0:T(8,128)S(1)}, s32[16,128]{1,0:T(8,128)}, u32[]{:S(2)}) copy-start(s32[16,128]{1,0:T(8,128)} %mask_ref.1) | copy-start | bytes 24580
  2.9 5.2 %collective-permute-start = (f32[16,8,128]{2,1,0:T(8,128)S(1)}, f32[16,8,128]{2,1,0:T(8,128)S(1)}, u32[]{:S(2)}, u32[]{:S(2)}) collective-permute-start(f32[16,8,128]{2,1,0:T(8,128)S(1)} %get-tuple-element.13), channel_id=1, source_target_pairs={{0,1},{1,0},{2,3},{3,2},{4,5},{5,4},{6,7},{7,6},{8,9},{9,8},{10,11... | collective-permute-start | bytes 196616 | tf_op jit(solution)/shard_map/ppermute | solution.py:595
  8.2 5.3 %collective-permute-start.2 = (f32[5,152,128]{2,1,0:T(8,128)S(1)}, f32[5,152,128]{2,1,0:T(8,128)S(1)}, u32[]{:S(2)}, u32[]{:S(2)}) collective-permute-start(f32[5,152,128]{2,1,0:T(8,128)S(1)} %get-tuple-element.16), channel_id=1, source_target_pairs={{0,2},{2,0},{4,6},{6,4},{8,10},{10,8},{12,14},{14,12},{16,18},{18,... | collective-permute-start | bytes 1167368 | tf_op jit(solution)/shard_map/ppermute | solution.py:603
  8.3 16.7 %collective-permute-start.1 = (f32[5,152,128]{2,1,0:T(8,128)S(1)}, f32[5,152,128]{2,1,0:T(8,128)S(1)}, u32[]{:S(2)}, u32[]{:S(2)}) collective-permute-start(f32[5,152,128]{2,1,0:T(8,128)S(1)} %get-tuple-element.15), channel_id=1, source_target_pairs={{0,30},{2,4},{4,2},{6,8},{8,6},{10,12},{12,10},{14,16},{16,14},{18... | collective-permute-start | bytes 1167368 | tf_op jit(solution)/shard_map/ppermute | solution.py:600
  30.2 1.3 %collective-permute-start.3 = (f32[2,64,128]{2,1,0:T(8,128)S(1)}, f32[2,64,128]{2,1,0:T(8,128)S(1)}, u32[]{:S(2)}, u32[]{:S(2)}) collective-permute-start(f32[2,64,128]{2,1,0:T(8,128)S(1)} %get-tuple-element.29), channel_id=1, source_target_pairs={{0,2},{1,3},{2,0},{3,1},{4,6},{5,7},{6,4},{7,5},{8,10},{9,11},{10,... | collective-permute-start | bytes 196616 | tf_op jit(solution)/shard_map/ppermute | solution.py:566
  31.6 4.3 %collective-permute-start.4 = (f32[2,64,128]{2,1,0:T(8,128)S(1)}, f32[2,64,128]{2,1,0:T(8,128)S(1)}, u32[]{:S(2)}, u32[]{:S(2)}) collective-permute-start(f32[2,64,128]{2,1,0:T(8,128)S(1)} %pad_maximum_fusion), channel_id=1, source_target_pairs={{0,1},{1,0},{2,3},{3,2},{4,5},{5,4},{6,7},{7,6},{8,9},{9,8},{10,11... | collective-permute-start | bytes 196616 | tf_op jit(solution)/shard_map/ppermute | solution.py:566
  33.1 5.5 %collective-permute-start.5 = (f32[2,64,128]{2,1,0:T(8,128)S(1)}, f32[2,64,128]{2,1,0:T(8,128)S(1)}, u32[]{:S(2)}, u32[]{:S(2)}) collective-permute-start(f32[2,64,128]{2,1,0:T(8,128)S(1)} %pad_maximum_fusion), channel_id=1, source_target_pairs={{0,4},{1,5},{2,6},{3,7},{4,0},{5,1},{6,2},{7,3},{8,12},{9,13},{10,... | collective-permute-start | bytes 196616 | tf_op jit(solution)/shard_map/ppermute | solution.py:566
  33.1 5.5 %collective-permute-start.6 = (f32[2,64,128]{2,1,0:T(8,128)S(1)}, f32[2,64,128]{2,1,0:T(8,128)S(1)}, u32[]{:S(2)}, u32[]{:S(2)}) collective-permute-start(f32[2,64,128]{2,1,0:T(8,128)S(1)} %pad_maximum_fusion), channel_id=1, source_target_pairs={{0,5},{1,4},{2,7},{3,6},{4,1},{5,0},{6,3},{7,2},{8,13},{9,12},{10,... | collective-permute-start | bytes 196616 | tf_op jit(solution)/shard_map/ppermute | solution.py:566
  38.7 4.5 %collective-permute-start.7 = (f32[2,64,128]{2,1,0:T(8,128)S(1)}, f32[2,64,128]{2,1,0:T(8,128)S(1)}, u32[]{:S(2)}, u32[]{:S(2)}) collective-permute-start(f32[2,64,128]{2,1,0:T(8,128)S(1)} %pad_maximum_fusion.1), channel_id=1, source_target_pairs={{0,8},{1,9},{2,10},{3,11},{4,12},{5,13},{6,14},{7,15},{8,0},{9,1},... | collective-permute-start | bytes 196616 | tf_op jit(solution)/shard_map/ppermute | solution.py:566
  38.7 5.9 %collective-permute-start.8 = (f32[2,64,128]{2,1,0:T(8,128)S(1)}, f32[2,64,128]{2,1,0:T(8,128)S(1)}, u32[]{:S(2)}, u32[]{:S(2)}) collective-permute-start(f32[2,64,128]{2,1,0:T(8,128)S(1)} %pad_maximum_fusion.1), channel_id=1, source_target_pairs={{0,16},{1,17},{2,18},{3,19},{4,20},{5,21},{6,22},{7,23},{8,24},{9,... | collective-permute-start | bytes 196616 | tf_op jit(solution)/shard_map/ppermute | solution.py:566
  41.1 6.1 %collective-permute-start.9 = (f32[2,64,128]{2,1,0:T(8,128)S(1)}, f32[2,64,128]{2,1,0:T(8,128)S(1)}, u32[]{:S(2)}, u32[]{:S(2)}) collective-permute-start(f32[2,64,128]{2,1,0:T(8,128)S(1)} %pad_maximum_fusion.1), channel_id=1, source_target_pairs={{0,24},{1,25},{2,26},{3,27},{4,28},{5,29},{6,30},{7,31},{8,16},{9,... | collective-permute-start | bytes 196616 | tf_op jit(solution)/shard_map/ppermute | solution.py:566
  47.2 1.3 %collective-permute-start.10 = (f32[2,64,128]{2,1,0:T(8,128)S(1)}, f32[2,64,128]{2,1,0:T(8,128)S(1)}, u32[]{:S(2)}, u32[]{:S(2)}) collective-permute-start(f32[2,64,128]{2,1,0:T(8,128)S(1)} %get-tuple-element.31), channel_id=1, source_target_pairs={{0,2},{1,3},{2,0},{3,1},{4,6},{5,7},{6,4},{7,5},{8,10},{9,11},{10,... | collective-permute-start | bytes 196616 | tf_op jit(solution)/shard_map/ppermute | solution.py:566
where the time goes:
time: 62.8 us; the launch traced here: 62.6 us
  Pallas kernels  30.9 us (49%)
  starting transfers between devices  16.4 us (26%)
  waiting for transfers between devices  12.3 us (20%)
  local copies, waits for them, and re-layouts  1.91 us (3%)
  between operations  0.91 us (1%)
    pallas_call x1, Pallas kernels, orthonormal(): pl.pallas_call(functools.partial(modes_kernel, clon=clon, clat=clat, snap...  13.8 us
    pallas_call x1, Pallas kernels, near_part(): pl.pallas_call(functools.partial(near_kernel, clon=clon, clat=clat, snaps...  11.5 us
    ppermute x8, waiting for transfers between devices, partner(): return lax.ppermute(value, BOTH, [(i, i ^ step) for i in range(count)])  10 us
    ppermute x8, starting transfers between devices, partner(): return lax.ppermute(value, BOTH, [(i, i ^ step) for i in range(count)])  8.14 us
    ppermute x1, starting transfers between devices, on_device(): lax.ppermute(far, 'lon', [(i, (i + 1 if i % 2 else i - 1) % nlon) for i i...  5.19 us
    pallas_call x1, Pallas kernels, far_part(): pl.pallas_call(functools.partial(far_kernel, clon=clon, clat=clat, snaps=...  5.15 us
    ppermute x1, starting transfers between devices, on_device(): left = right = lax.ppermute(edges[0], 'lat', [(0, 1), (1, 0)])  3 us
    ppermute x1, waiting for transfers between devices, on_device(): left = right = lax.ppermute(edges[0], 'lat', [(0, 1), (1, 0)])  2.25 us
  transfers between devices with their start and end apart: 11, of which 7 were waited for; matrix products, arithmetic and copies ran while one was open for 0% of the time, Pallas kernels for 18%

commit v1 on v0

--- a/solution.py
+++ b/solution.py
@@ -10,6 +10,7 @@
 PASSES = 4
 HALO = PASSES + 1
 EDGE = 8
+NEAR_ONE = 2.0**-6
 ROUND = 1.5 * 2.0**23
 BOTH = ("lon", "lat")
 HIGHEST = lax.Precision.HIGHEST
@@ -68,7 +69,7 @@
     for row in range(clon):
         spot = longitude(backwards, row, clon)
         plane = pressure_ref[pl.ds(spot, snaps, stride=clon), :].T
-        mask = mask_ref[pl.ds(spot, 1), :].astype(jnp.float32)
+        mask = mask_ref[pl.ds(spot, 1), :]
         turned_ref[row] = plane
         mask_out_ref[row : row + 1] = mask
         low = jnp.where(line < HALO, plane[:EDGE], mask)
@@ -199,16 +200,11 @@
         swept[row, EDGE + tall :] = zeros
 
 
-def fields_of(backwards, tables, source, planes, x_ref, sems, rows, offset, clon, clat, snaps):
+def fields_of(backwards, tables, source, planes, rows, offset, clat, snaps):
     begin = 2 * EDGE
     end = begin + clat
     count = len(rows)
     sign = jnp.where(backwards > 0, -2.0, 2.0)
-
-    def copy(which, i):
-        spot = which * count + i
-        to = which * clon + longitude(backwards, rows[0] + i, clon)
-        return pltpu.make_async_copy(planes.at[spot], x_ref.at[to], sems.at[spot])
 
     def one(i, top):
         here = rows[0] + i + offset
@@ -222,21 +218,9 @@
             value = value.T
             planes[which * count + i] = value
             top = jnp.maximum(top, jnp.abs(value))
-        for which in range(3):
-            copy(which, i).start()
         return top
 
-    top = lax.fori_loop(0, count, one, jnp.zeros((snaps, clat), jnp.float32))
-
-    def finish():
-        def wait(i, carry):
-            for which in range(3):
-                copy(which, i).wait()
-            return carry
-
-        lax.fori_loop(0, count, wait, 0)
-
-    return top, finish
+    return lax.fori_loop(0, count, one, jnp.zeros((snaps, clat), jnp.float32))
 
 
 def gram_of(planes, count, top, snaps, clat):
@@ -285,7 +269,7 @@
 
 def near_kernel(
     turned_ref, mask_ref, left_ref, right_ref, near_ref, x_ref, rim_ref, gram_ref,
-    field_a, field_b, swept, masks, keep_lon, keep_lat, quarter, planes, sems, *, clon, clat, snaps,
+    field_a, field_b, swept, masks, keep_lon, keep_lat, quarter, *, clon, clat, snaps,
 ):
     tall = clat + 2 * EDGE
     lower, upper = EDGE, EDGE + tall
@@ -324,14 +308,13 @@
             sweep(tables, source, target, swept, step + 1, wide - 1 - step, tall)
             source, target = target, source
     rows = range(clon - HALO)
-    top, finish = fields_of(backwards, tables, source, planes, x_ref, sems, rows, HALO, clon, clat, snaps)
-    put_gram(gram_ref, *gram_of(planes, 3 * len(rows), top, snaps, clat))
-    finish()
+    top = fields_of(backwards, tables, source, x_ref, rows, HALO, clat, snaps)
+    put_gram(gram_ref, *gram_of(x_ref, 3 * len(rows), top, snaps, clat))
 
 
 def far_kernel(
-    mask_ref, left_ref, right_ref, far_ref, rim_ref, gram_in_ref, x_in_ref, x_ref, gram_ref,
-    field_a, field_b, swept, masks, keep_lon, keep_lat, quarter, planes, sems, *, clon, clat, snaps,
+    mask_ref, left_ref, right_ref, far_ref, rim_ref, gram_in_ref, x_ref, gram_ref,
+    field_a, field_b, swept, masks, keep_lon, keep_lat, quarter, *, clon, clat, snaps,
 ):
     tall = clat + 2 * EDGE
     lower, upper = EDGE, EDGE + tall
@@ -360,56 +343,48 @@
             sweep(tables, source, target, swept, HALO - step, 2 * HALO - step, tall)
             source, target = target, source
     rows = range(clon - HALO, clon)
-    top, finish = fields_of(backwards, tables, source, planes, x_ref, sems, rows, -skip, clon, clat, snaps)
-    gram = gram_of(planes, 3 * len(rows), top, snaps, clat)
+    top = fields_of(backwards, tables, source, x_ref, rows, -skip, clat, snaps)
+    gram = gram_of(x_ref, 3 * len(rows), top, snaps, clat)
     before = [jnp.concatenate([gram_in_ref[0, part], gram_in_ref[1, part]], axis=0) for part in range(2)]
     put_gram(gram_ref, *add_pairs(before, gram))
-    finish()
-
-
-def filter_scratch(wide, planes, clat, snaps):
+
+
+def filter_scratch(wide, clat, snaps):
     tall = clat + 2 * EDGE
     field = pltpu.VMEM((wide, tall + 2 * EDGE, snaps), jnp.float32)
     table = pltpu.VMEM((wide, tall, snaps), jnp.float32)
     masks = pltpu.VMEM((3, -(-wide // 8) * 8, clat), jnp.float32)
-    return [
-        field, field, field, masks, table, table, table,
-        pltpu.VMEM((planes, snaps, clat), jnp.float32),
-        pltpu.SemaphoreType.DMA((planes,)),
-    ]
+    return [field, field, field, masks, table, table, table]
 
 
 def near_part(turned, mask, left, right, near):
     clon, clat, snaps = turned.shape
-    planes = 3 * (clon - HALO)
     return pl.pallas_call(
         functools.partial(near_kernel, clon=clon, clat=clat, snaps=snaps),
         out_shape=[
-            f32(3 * clon, snaps, clat),
+            f32(3 * (clon - HALO), snaps, clat),
             f32(PASSES + 1, 2, clat + 2 * EDGE, snaps),
             f32(2, 2, snaps // 2, snaps),
         ],
         in_specs=[VMEM] * 5,
-        out_specs=[ANYWHERE, VMEM, VMEM],
-        scratch_shapes=filter_scratch(clon + HALO, planes, clat, snaps),
+        out_specs=[VMEM, VMEM, VMEM],
+        scratch_shapes=filter_scratch(clon + HALO, clat, snaps),
         compiler_params=PARAMS,
         cost_estimate=pl.CostEstimate(flops=4_000_000_000, bytes_accessed=8_000_000, transcendentals=0),
         name="near_part",
     )(turned, mask, left, right, near)
 
 
-def far_part(mask, left, right, far, rim, gram, x, clon, clat, snaps):
-    planes = 3 * HALO
+def far_part(mask, left, right, far, rim, gram, clon, clat, snaps):
     return pl.pallas_call(
         functools.partial(far_kernel, clon=clon, clat=clat, snaps=snaps),
-        out_shape=[f32(3 * clon, snaps, clat), f32(2, 2, snaps // 2, snaps)],
-        in_specs=[VMEM] * 6 + [ANYWHERE],
-        out_specs=[ANYWHERE, VMEM],
-        scratch_shapes=filter_scratch(2 * HALO + 1, planes, clat, snaps),
-        input_output_aliases={6: 0},
+        out_shape=[f32(3 * HALO, snaps, clat), f32(2, 2, snaps // 2, snaps)],
+        in_specs=[VMEM] * 6,
+        out_specs=[VMEM, VMEM],
+        scratch_shapes=filter_scratch(2 * HALO + 1, clat, snaps),
         compiler_params=PARAMS,
         name="far_part",
-    )(mask, left, right, far, rim, gram, x)
+    )(mask, left, right, far, rim, gram)
 
 
 def spread(row, lane):
@@ -472,9 +447,9 @@
     return first, second, third
 
 
-def modes_kernel(gram_ref, x_ref, modes_ref, factor_ref, x_vmem, out_vmem, in_sem, out_sems, *, clon, clat, snaps, total_rows):
-    load = pltpu.make_async_copy(x_ref, x_vmem, in_sem)
-    load.start()
+def modes_kernel(
+    gram_ref, near_ref, far_ref, modes_ref, factor_ref, out_vmem, upper_vmem, combined_vmem, out_sems, *, clon, clat, snaps, total_rows
+):
     head, tail = [jnp.concatenate([gram_ref[0, part], gram_ref[1, part]], axis=0) for part in range(2)]
     row = lax.broadcasted_iota(jnp.int32, (snaps, snaps), 0)
     col = lax.broadcasted_iota(jnp.int32, (snaps, snaps), 1)
@@ -506,56 +481,89 @@
     left_over = dot_nn(dot_nn(inverse_one, missing, HIGHEST), inverse_one.T, HIGHEST)
     gram_two = dot_nn(near_one, near_one.T, HIGHEST) + left_over
     gram_two = 0.5 * (gram_two + gram_two.T)
-    upper_two, inverse_two = eliminate(gram_two)
+    difference = gram_two - jnp.where(row == col, 1.0, 0.0)
+
+    def lower_half(matrix):
+        return jnp.where(row > col, matrix, jnp.where(row == col, 0.5 * matrix, 0.0))
+
+    small = jnp.sum(difference * difference) < NEAR_ONE**2
+
+    @pl.when(small)
+    def _():
+        k = lower_half(difference)
+        for _ in range(2):
+            rough = k.astype(jnp.bfloat16)
+            k = lower_half(difference - dot_nt(rough, rough))
+        rough = k.astype(jnp.bfloat16)
+        square = dot_nn(rough, rough)
+        change = k - dot_nn(rough, (k - square).astype(jnp.bfloat16))
+        upper_vmem[...] = k.T + jnp.where(row == col, 1.0, 0.0)
+        combined_vmem[...] = inverse_one - dot_nn(change, inverse_one, HIGHEST)
+
+    @pl.when(jnp.logical_not(small))
+    def _():
+        upper, inverse = eliminate(gram_two)
+        upper_vmem[...] = upper
+        combined_vmem[...] = dot_nn(inverse, inverse_one, HIGHEST)
 
     scale = float(total_rows) ** 0.5
-    combined = dot_nn(inverse_two, inverse_one, HIGHEST) * shrink_cols * scale
+    combined = combined_vmem[...] * shrink_cols * scale
     first, second, third = thirds(combined)
     first_second = jnp.concatenate([first, second], axis=1)
     first_third = jnp.concatenate([first, third], axis=1)
-    load.wait()
+    backwards, _, _, _ = place()
+    near_rows = clon - HALO
+
+    def plane(which, q):
+        if q < near_rows:
+            return near_ref[which * near_rows + q]
+        return far_ref[which * HALO + q - near_rows]
+
     copies = []
     for which in range(3):
         for part in range(clon // 8):
             spot = which * (clon // 8) + part
             flat = out_vmem.at[spot].reshape(snaps * 8, clat)
             for lon in range(0, 8, 2):
-                plane = which * clon + part * 8 + lon
-                x_one, x_two, x_three = thirds(jnp.concatenate([x_vmem[plane], x_vmem[plane + 1]], axis=1))
+                q = part * 8 + lon
+                both = jnp.concatenate([plane(which, q), plane(which, q + 1)], axis=1)
+                x_one, x_two, x_three = thirds(both)
                 value = (
                     dot_nn(first_third, jnp.concatenate([x_three, x_one], axis=0))
                     + dot_nn(first_second, jnp.concatenate([x_two, x_two], axis=0))
                 ) + dot_nn(first_second, jnp.concatenate([x_one, x_one], axis=0))
-                flat[pl.ds(lon, snaps, stride=8), :] = value[:, :clat]
-                flat[pl.ds(lon + 1, snaps, stride=8), :] = value[:, clat:]
+                for side in range(2):
+                    to = longitude(backwards, lon + side, 8)
+                    flat[pl.ds(to, snaps, stride=8), :] = value[:, side * clat : (side + 1) * clat]
+            to = pl.multiple_of(8 * longitude(backwards, part, clon // 8), 8)
             copy = pltpu.make_async_copy(
-                out_vmem.at[spot], modes_ref.at[:, which, pl.ds(part * 8, 8), :], out_sems.at[spot]
+                out_vmem.at[spot], modes_ref.at[:, which, pl.ds(to, 8), :], out_sems.at[spot]
             )
             copy.start()
             copies.append(copy)
-    factor = dot_nn(upper_two, lower_one.T, HIGHEST) * jnp.broadcast_to(grow, (snaps, snaps)).T
+    factor = dot_nn(upper_vmem[...], lower_one.T, HIGHEST) * jnp.broadcast_to(grow, (snaps, snaps)).T
     factor_ref[...] = jnp.where(col >= row, factor * (1.0 / scale), 0.0)
     for copy in copies:
         copy.wait()
 
 
-def orthonormal(gram, x, clon, clat, total_rows):
+def orthonormal(gram, x_near, x_far, clon, clat, total_rows):
     snaps = gram.shape[3]
     parts = 3 * clon // 8
     return pl.pallas_call(
         functools.partial(modes_kernel, clon=clon, clat=clat, snaps=snaps, total_rows=total_rows),
         out_shape=[f32(snaps, 3, clon, clat), f32(snaps, snaps)],
-        in_specs=[VMEM, ANYWHERE],
+        in_specs=[VMEM] * 3,
         out_specs=[ANYWHERE, VMEM],
         scratch_shapes=[
-            pltpu.VMEM((3 * clon, snaps, clat), jnp.float32),
             pltpu.VMEM((parts, snaps, 8, clat), jnp.float32),
-            pltpu.SemaphoreType.DMA,
+            pltpu.VMEM((snaps, snaps), jnp.float32),
+            pltpu.VMEM((snaps, snaps), jnp.float32),
             pltpu.SemaphoreType.DMA((parts,)),
         ],
         compiler_params=PARAMS,
         name="orthonormal",
-    )(gram, x)
+    )(gram, x_near, x_far)
 
 
 def summed(halves, nlon, nlat):
@@ -590,7 +598,7 @@
     snaps, clon, clat = pressure.shape
     nlon, nlat = lax.axis_size("lon"), lax.axis_size("lat")
     merged = nlat == 2
-    turned, mask, *edges = prepare(pressure, ocean_mask, 1 if merged else 2)
+    turned, mask, *edges = prepare(pressure, ocean_mask.astype(jnp.float32), 1 if merged else 2)
     if merged:
         left = right = lax.ppermute(edges[0], "lat", [(0, 1), (1, 0)])
     else:
@@ -601,10 +609,10 @@
         far, "lon", [(i, (i + 1 if i % 2 else i - 1) % nlon) for i in range(nlon)]
     )
     near = lax.ppermute(near, "lon", [(i, i ^ 1) for i in range(nlon)])
-    x, rim, gram = near_part(turned, mask, left, right, near)
-    x, gram = far_part(mask, left, right, far, rim, gram, x, clon, clat, snaps)
+    x_near, rim, gram = near_part(turned, mask, left, right, near)
+    x_far, gram = far_part(mask, left, right, far, rim, gram, clon, clat, snaps)
     gram = summed(gram, nlon, nlat)
-    return tuple(orthonormal(gram, x, clon, clat, 3 * clon * clat * nlon * nlat))
+    return tuple(orthonormal(gram, x_near, x_far, clon, clat, 3 * clon * clat * nlon * nlat))
 
 
 def solution(mesh):

time: 62.8 us -> 54.4 us (0.87)
  Pallas kernels: 30.9 us -> 22.7 us
  other arithmetic: 0.13 us -> 0.83 us
  local copies, waits for them, and re-layouts: 1.91 us -> 1.22 us
    pallas_call x1, Pallas kernels: 13.8 us -> 10.2 us  [orthonormal(): pl.pallas_call(functools.partial(modes_kernel, clon=clon, clat=clat, snap...]
    pallas_call x1, Pallas kernels: 11.5 us -> 8.36 us  [near_part(): pl.pallas_call(functools.partial(near_kernel, clon=clon, clat=clat, snaps...]
    pallas_call x1, Pallas kernels: 5.15 us -> 3.71 us  [far_part(): pl.pallas_call(functools.partial(far_kernel, clon=clon, clat=clat, snaps=...]
    convert_element_type x0 -> x1, other arithmetic: none -> 0.7 us  [on_device(): ocean_mask.astype(jnp.float32)]
    unnamed x4 -> x2, local copies, waits for them, and re-layouts: 1.91 us -> 1.22 us
  transfers between devices with their start and end apart: 11 -> 11, of which waited for: 7 -> 8; matrix products, arithmetic and copies ran while one was open for 0% -> 0% of each run, Pallas kernels for 18% -> 15%
where the time goes in v1:
time: 54.4 us; the launch traced here: 54.2 us
  Pallas kernels  22.7 us (42%)
  starting transfers between devices  16.4 us (30%)
  waiting for transfers between devices  12.1 us (22%)
  local copies, waits for them, and re-layouts  1.22 us (2%)
  between operations  0.89 us (2%)
  other arithmetic  0.83 us (2%)
    pallas_call x1, Pallas kernels, orthonormal(): pl.pallas_call(functools.partial(modes_kernel, clon=clon, clat=clat, snap...  10.2 us
    ppermute x8, waiting for transfers between devices, partner(): return lax.ppermute(value, BOTH, [(i, i ^ step) for i in range(count)])  9.86 us
    pallas_call x1, Pallas kernels, near_part(): pl.pallas_call(functools.partial(near_kernel, clon=clon, clat=clat, snaps...  8.36 us
    ppermute x8, starting transfers between devices, partner(): return lax.ppermute(value, BOTH, [(i, i ^ step) for i in range(count)])  8.15 us
    ppermute x1, starting transfers between devices, on_device(): lax.ppermute(far, 'lon', [(i, (i + 1 if i % 2 else i - 1) % nlon) for i i...  5.19 us
    pallas_call x1, Pallas kernels, far_part(): pl.pallas_call(functools.partial(far_kernel, clon=clon, clat=clat, snaps=...  3.71 us
    ppermute x1, starting transfers between devices, on_device(): left = right = lax.ppermute(edges[0], 'lat', [(0, 1), (1, 0)])  3 us
    ppermute x1, waiting for transfers between devices, on_device(): left = right = lax.ppermute(edges[0], 'lat', [(0, 1), (1, 0)])  2.25 us
  transfers between devices with their start and end apart: 11, of which 8 were waited for; matrix products, arithmetic and copies ran while one was open for 0% of the time, Pallas kernels for 15%

profile of v1, /device:TPU:0, one launch (start us, length us, event | category | flops | bytes accessed | tf_op | source)
XLA Modules:
  0.0 54.2 jit_solution(9066353913568143479)
XLA Ops:
  0.6 0.7 %convert_element_type.3.mask_ref = f32[16,128]{1,0:T(8,128)S(1)} convert(s32[16,128]{1,0:T(8,128)} %param.3) | non-fusion elementwise | flops 2048 | bytes 16384 | tf_op jit(solution)/shard_map/convert_element_type | solution.py:601
  1.3 1.2 %copy-done = f32[128,16,128]{2,1,0:T(8,128)S(1)} copy-done((f32[128,16,128]{2,1,0:T(8,128)S(1)}, f32[128,16,128]{2,1,0:T(8,128)}, u32[]{:S(2)}) %copy-start) | copy-done | bytes 1048600
  2.6 0.4 prepare.1
  2.9 3.0 %collective-permute-start = (f32[16,8,128]{2,1,0:T(8,128)S(1)}, f32[16,8,128]{2,1,0:T(8,128)S(1)}, u32[]{:S(2)}, u32[]{:S(2)}) collective-permute-start(f32[16,8,128]{2,1,0:T(8,128)S(1)} %get-tuple-element.13), channel_id=1, source_target_pairs={{0,1},{1,0},{2,3},{3,2},{4,5},{5,4},{6,7},{7,6},{8,9},{9,8},{10,11... | collective-permute-start | bytes 196616 | tf_op jit(solution)/shard_map/ppermute | solution.py:603
  5.9 2.2 %collective-permute-done.left_ref.right_ref = f32[16,8,128]{2,1,0:T(8,128)S(1)} collective-permute-done((f32[16,8,128]{2,1,0:T(8,128)S(1)}, f32[16,8,128]{2,1,0:T(8,128)S(1)}, u32[]{:S(2)}, u32[]{:S(2)}) %collective-permute-start) | collective-permute-done | bytes 65568 | tf_op jit(solution)/shard_map/ppermute | solution.py:603
  8.2 0.1 collective-permute-start.2
  8.3 5.2 %collective-permute-start.1 = (f32[5,152,128]{2,1,0:T(8,128)S(1)}, f32[5,152,128]{2,1,0:T(8,128)S(1)}, u32[]{:S(2)}, u32[]{:S(2)}) collective-permute-start(f32[5,152,128]{2,1,0:T(8,128)S(1)} %get-tuple-element.15), channel_id=1, source_target_pairs={{0,30},{2,4},{4,2},{6,8},{8,6},{10,12},{12,10},{14,16},{16,14},{18... | collective-permute-start | bytes 1167368 | tf_op jit(solution)/shard_map/ppermute | solution.py:608
  13.5 8.4 %near_part.1 = (f32[33,128,128]{2,1,0:T(8,128)S(1)}, f32[5,2,144,128]{3,2,1,0:T(8,128)S(1)}, f32[2,2,64,128]{3,2,1,0:T(8,128)S(1)}) custom-call(f32[16,128,128]{2,1,0:T(8,128)S(1)} %get-tuple-element.14.turned_ref, f32[16,128]{1,0:T(8,128)S(1)} %get-tuple-element.12.mask_ref, f32[16,8,128]{2,1,0:T(8,128)S(1)} %collective-permute-done.left_ref.right_ref, ...), custom_call_target="tpu_custom_call" | custom-call | flops 4000000000 | bytes 8000000 | tf_op jit(solution)/shard_map/near_part/pallas_call | solution.py:362
  21.9 3.7 %far_part.1 = (f32[15,128,128]{2,1,0:T(8,128)S(1)}, f32[2,2,64,128]{3,2,1,0:T(8,128)S(1)}) custom-call(f32[16,128]{1,0:T(8,128)S(1)} %get-tuple-element.12.mask_ref, f32[16,8,128]{2,1,0:T(8,128)S(1)} %collective-permute-done.left_ref.right_ref, f32[16,8,128]{2,1,0:T(8,128)S(1)} %collective-permute-done.left_ref.right_ref, ...), custom_call_target="tpu_custom_call" | custom-call | tf_op jit(solution)/shard_map/far_part/pallas_call | solution.py:379
  25.6 0.1 collective-permute-start.3
  25.7 1.2 %collective-permute-done.3 = f32[2,64,128]{2,1,0:T(8,128)S(1)} collective-permute-done((f32[2,64,128]{2,1,0:T(8,128)S(1)}, f32[2,64,128]{2,1,0:T(8,128)S(1)}, u32[]{:S(2)}, u32[]{:S(2)}) %collective-permute-start.3) | collective-permute-done | bytes 65568 | tf_op jit(solution)/shard_map/ppermute | solution.py:574
  27.0 0.9 %collective-permute-start.6 = (f32[2,64,128]{2,1,0:T(8,128)S(1)}, f32[2,64,128]{2,1,0:T(8,128)S(1)}, u32[]{:S(2)}, u32[]{:S(2)}) collective-permute-start(f32[2,64,128]{2,1,0:T(8,128)S(1)} %pad_maximum_fusion), channel_id=1, source_target_pairs={{0,5},{1,4},{2,7},{3,6},{4,1},{5,0},{6,3},{7,2},{8,13},{9,12},{10,... | collective-permute-start | bytes 196616 | tf_op jit(solution)/shard_map/ppermute | solution.py:574
  27.9 2.2 %collective-permute-start.5 = (f32[2,64,128]{2,1,0:T(8,128)S(1)}, f32[2,64,128]{2,1,0:T(8,128)S(1)}, u32[]{:S(2)}, u32[]{:S(2)}) collective-permute-start(f32[2,64,128]{2,1,0:T(8,128)S(1)} %pad_maximum_fusion), channel_id=1, source_target_pairs={{0,4},{1,5},{2,6},{3,7},{4,0},{5,1},{6,2},{7,3},{8,12},{9,13},{10,... | collective-permute-start | bytes 196616 | tf_op jit(solution)/shard_map/ppermute | solution.py:574
  30.0 0.5 collective-permute-start.4
  30.5 2.1 %collective-permute-done.6 = f32[2,64,128]{2,1,0:T(8,128)S(1)} collective-permute-done((f32[2,64,128]{2,1,0:T(8,128)S(1)}, f32[2,64,128]{2,1,0:T(8,128)S(1)}, u32[]{:S(2)}, u32[]{:S(2)}) %collective-permute-start.6) | collective-permute-done | bytes 65568 | tf_op jit(solution)/shard_map/ppermute | solution.py:574
  32.6 0.9 %collective-permute-done.5 = f32[2,64,128]{2,1,0:T(8,128)S(1)} collective-permute-done((f32[2,64,128]{2,1,0:T(8,128)S(1)}, f32[2,64,128]{2,1,0:T(8,128)S(1)}, u32[]{:S(2)}, u32[]{:S(2)}) %collective-permute-start.5) | collective-permute-done | bytes 65568 | tf_op jit(solution)/shard_map/ppermute | solution.py:574
  33.5 0.8 %collective-permute-done.4 = f32[2,64,128]{2,1,0:T(8,128)S(1)} collective-permute-done((f32[2,64,128]{2,1,0:T(8,128)S(1)}, f32[2,64,128]{2,1,0:T(8,128)S(1)}, u32[]{:S(2)}, u32[]{:S(2)}) %collective-permute-start.4) | collective-permute-done | bytes 65568 | tf_op jit(solution)/shard_map/ppermute | solution.py:574
  34.3 2.1 %collective-permute-start.9 = (f32[2,64,128]{2,1,0:T(8,128)S(1)}, f32[2,64,128]{2,1,0:T(8,128)S(1)}, u32[]{:S(2)}, u32[]{:S(2)}) collective-permute-start(f32[2,64,128]{2,1,0:T(8,128)S(1)} %pad_maximum_fusion.1), channel_id=1, source_target_pairs={{0,24},{1,25},{2,26},{3,27},{4,28},{5,29},{6,30},{7,31},{8,16},{9,... | collective-permute-start | bytes 196616 | tf_op jit(solution)/shard_map/ppermute | solution.py:574
  36.4 2.3 %collective-permute-start.7 = (f32[2,64,128]{2,1,0:T(8,128)S(1)}, f32[2,64,128]{2,1,0:T(8,128)S(1)}, u32[]{:S(2)}, u32[]{:S(2)}) collective-permute-start(f32[2,64,128]{2,1,0:T(8,128)S(1)} %pad_maximum_fusion.1), channel_id=1, source_target_pairs={{0,8},{1,9},{2,10},{3,11},{4,12},{5,13},{6,14},{7,15},{8,0},{9,1},... | collective-permute-start | bytes 196616 | tf_op jit(solution)/shard_map/ppermute | solution.py:574
  38.8 2.4 %collective-permute-done.9 = f32[2,64,128]{2,1,0:T(8,128)S(1)} collective-permute-done((f32[2,64,128]{2,1,0:T(8,128)S(1)}, f32[2,64,128]{2,1,0:T(8,128)S(1)}, u32[]{:S(2)}, u32[]{:S(2)}) %collective-permute-start.9) | collective-permute-done | bytes 65568 | tf_op jit(solution)/shard_map/ppermute | solution.py:574
  41.2 1.3 %collective-permute-done.8 = f32[2,64,128]{2,1,0:T(8,128)S(1)} collective-permute-done((f32[2,64,128]{2,1,0:T(8,128)S(1)}, f32[2,64,128]{2,1,0:T(8,128)S(1)}, u32[]{:S(2)}, u32[]{:S(2)}) %collective-permute-start.8) | collective-permute-done | bytes 65568 | tf_op jit(solution)/shard_map/ppermute | solution.py:574
  42.5 0.1 collective-permute-start.10
  42.6 1.2 %collective-permute-done.10 = f32[2,64,128]{2,1,0:T(8,128)S(1)} collective-permute-done((f32[2,64,128]{2,1,0:T(8,128)S(1)}, f32[2,64,128]{2,1,0:T(8,128)S(1)}, u32[]{:S(2)}, u32[]{:S(2)}) %collective-permute-start.10) | collective-permute-done | bytes 65568 | tf_op jit(solution)/shard_map/ppermute | solution.py:574
  43.8 10.2 %orthonormal.1 = (f32[128,3,16,128]{3,2,1,0:T(8,128)}, f32[128,128]{1,0:T(8,128)}) custom-call(f32[2,2,64,128]{3,2,1,0:T(8,128)S(1)} %maximum_select_fusion.gram_ref, f32[33,128,128]{2,1,0:T(8,128)S(1)} %get-tuple-element.20.near_ref, f32[15,128,128]{2,1,0:T(8,128)S(1)} %get-tuple-element.21.far_ref), custom_call_target="tpu_custom_call" | custom-call | tf_op jit(solution)/shard_map/orthonormal/pallas_call | solution.py:553
  (14 shorter events, 0.2 us)
Async XLA Ops:
  1.3 1.2 %copy-start = (f32[128,16,128]{2,1,0:T(8,128)S(1)}, f32[128,16,128]{2,1,0:T(8,128)}, u32[]{:S(2)}) copy-start(f32[128,16,128]{2,1,0:T(8,128)} %param.2) | copy-start | bytes 3145732
  2.9 5.2 %collective-permute-start = (f32[16,8,128]{2,1,0:T(8,128)S(1)}, f32[16,8,128]{2,1,0:T(8,128)S(1)}, u32[]{:S(2)}, u32[]{:S(2)}) collective-permute-start(f32[16,8,128]{2,1,0:T(8,128)S(1)} %get-tuple-element.13), channel_id=1, source_target_pairs={{0,1},{1,0},{2,3},{3,2},{4,5},{5,4},{6,7},{7,6},{8,9},{9,8},{10,11... | collective-permute-start | bytes 196616 | tf_op jit(solution)/shard_map/ppermute | solution.py:603
  8.2 5.3 %collective-permute-start.2 = (f32[5,152,128]{2,1,0:T(8,128)S(1)}, f32[5,152,128]{2,1,0:T(8,128)S(1)}, u32[]{:S(2)}, u32[]{:S(2)}) collective-permute-start(f32[5,152,128]{2,1,0:T(8,128)S(1)} %get-tuple-element.16), channel_id=1, source_target_pairs={{0,2},{2,0},{4,6},{6,4},{8,10},{10,8},{12,14},{14,12},{16,18},{18,... | collective-permute-start | bytes 1167368 | tf_op jit(solution)/shard_map/ppermute | solution.py:611
  8.3 13.6 %collective-permute-start.1 = (f32[5,152,128]{2,1,0:T(8,128)S(1)}, f32[5,152,128]{2,1,0:T(8,128)S(1)}, u32[]{:S(2)}, u32[]{:S(2)}) collective-permute-start(f32[5,152,128]{2,1,0:T(8,128)S(1)} %get-tuple-element.15), channel_id=1, source_target_pairs={{0,30},{2,4},{4,2},{6,8},{8,6},{10,12},{12,10},{14,16},{16,14},{18... | collective-permute-start | bytes 1167368 | tf_op jit(solution)/shard_map/ppermute | solution.py:608
  25.6 1.3 %collective-permute-start.3 = (f32[2,64,128]{2,1,0:T(8,128)S(1)}, f32[2,64,128]{2,1,0:T(8,128)S(1)}, u32[]{:S(2)}, u32[]{:S(2)}) collective-permute-start(f32[2,64,128]{2,1,0:T(8,128)S(1)} %get-tuple-element.29), channel_id=1, source_target_pairs={{0,2},{1,3},{2,0},{3,1},{4,6},{5,7},{6,4},{7,5},{8,10},{9,11},{10,... | collective-permute-start | bytes 196616 | tf_op jit(solution)/shard_map/ppermute | solution.py:574
  27.0 5.6 %collective-permute-start.6 = (f32[2,64,128]{2,1,0:T(8,128)S(1)}, f32[2,64,128]{2,1,0:T(8,128)S(1)}, u32[]{:S(2)}, u32[]{:S(2)}) collective-permute-start(f32[2,64,128]{2,1,0:T(8,128)S(1)} %pad_maximum_fusion), channel_id=1, source_target_pairs={{0,5},{1,4},{2,7},{3,6},{4,1},{5,0},{6,3},{7,2},{8,13},{9,12},{10,... | collective-permute-start | bytes 196616 | tf_op jit(solution)/shard_map/ppermute | solution.py:574
  27.9 5.7 %collective-permute-start.5 = (f32[2,64,128]{2,1,0:T(8,128)S(1)}, f32[2,64,128]{2,1,0:T(8,128)S(1)}, u32[]{:S(2)}, u32[]{:S(2)}) collective-permute-start(f32[2,64,128]{2,1,0:T(8,128)S(1)} %pad_maximum_fusion), channel_id=1, source_target_pairs={{0,4},{1,5},{2,6},{3,7},{4,0},{5,1},{6,2},{7,3},{8,12},{9,13},{10,... | collective-permute-start | bytes 196616 | tf_op jit(solution)/shard_map/ppermute | solution.py:574
  30.0 4.3 %collective-permute-start.4 = (f32[2,64,128]{2,1,0:T(8,128)S(1)}, f32[2,64,128]{2,1,0:T(8,128)S(1)}, u32[]{:S(2)}, u32[]{:S(2)}) collective-permute-start(f32[2,64,128]{2,1,0:T(8,128)S(1)} %pad_maximum_fusion), channel_id=1, source_target_pairs={{0,1},{1,0},{2,3},{3,2},{4,5},{5,4},{6,7},{7,6},{8,9},{9,8},{10,11... | collective-permute-start | bytes 196616 | tf_op jit(solution)/shard_map/ppermute | solution.py:574
  34.3 6.8 %collective-permute-start.9 = (f32[2,64,128]{2,1,0:T(8,128)S(1)}, f32[2,64,128]{2,1,0:T(8,128)S(1)}, u32[]{:S(2)}, u32[]{:S(2)}) collective-permute-start(f32[2,64,128]{2,1,0:T(8,128)S(1)} %pad_maximum_fusion.1), channel_id=1, source_target_pairs={{0,24},{1,25},{2,26},{3,27},{4,28},{5,29},{6,30},{7,31},{8,16},{9,... | collective-permute-start | bytes 196616 | tf_op jit(solution)/shard_map/ppermute | solution.py:574
  36.4 6.0 %collective-permute-start.8 = (f32[2,64,128]{2,1,0:T(8,128)S(1)}, f32[2,64,128]{2,1,0:T(8,128)S(1)}, u32[]{:S(2)}, u32[]{:S(2)}) collective-permute-start(f32[2,64,128]{2,1,0:T(8,128)S(1)} %pad_maximum_fusion.1), channel_id=1, source_target_pairs={{0,16},{1,17},{2,18},{3,19},{4,20},{5,21},{6,22},{7,23},{8,24},{9,... | collective-permute-start | bytes 196616 | tf_op jit(solution)/shard_map/ppermute | solution.py:574
  36.4 6.0 %collective-permute-start.7 = (f32[2,64,128]{2,1,0:T(8,128)S(1)}, f32[2,64,128]{2,1,0:T(8,128)S(1)}, u32[]{:S(2)}, u32[]{:S(2)}) collective-permute-start(f32[2,64,128]{2,1,0:T(8,128)S(1)} %pad_maximum_fusion.1), channel_id=1, source_target_pairs={{0,8},{1,9},{2,10},{3,11},{4,12},{5,13},{6,14},{7,15},{8,0},{9,1},... | collective-permute-start | bytes 196616 | tf_op jit(solution)/shard_map/ppermute | solution.py:574
  42.5 1.3 %collective-permute-start.10 = (f32[2,64,128]{2,1,0:T(8,128)S(1)}, f32[2,64,128]{2,1,0:T(8,128)S(1)}, u32[]{:S(2)}, u32[]{:S(2)}) collective-permute-start(f32[2,64,128]{2,1,0:T(8,128)S(1)} %get-tuple-element.31), channel_id=1, source_target_pairs={{0,2},{1,3},{2,0},{3,1},{4,6},{5,7},{6,4},{7,5},{8,10},{9,11},{10,... | collective-permute-start | bytes 196616 | tf_op jit(solution)/shard_map/ppermute | solution.py:574

commit v2 on v1

--- a/solution.py
+++ b/solution.py
@@ -63,7 +63,10 @@
     return row + backwards * (clon - 1 - 2 * row)
 
 
-def prepare_kernel(pressure_ref, mask_ref, turned_ref, mask_out_ref, *edge_refs, clon, clat, snaps):
+def prepare_kernel(
+    pressure_ref, mask_ref, turned_ref, mask_out_ref, near_ref, far_ref, *end_refs, clon, clat, snaps
+):
+    edge_refs, near_edge_refs, far_edge_refs = [end_refs[i::3] for i in range(3)]
     backwards, lat, _, _ = place()
     line = lax.broadcasted_iota(jnp.int32, (EDGE, clat), 0)
     for row in range(clon):
@@ -77,6 +80,15 @@
         ends = (low, high) if len(edge_refs) == 2 else (jnp.where(lat == 0, high, low),)
         for edge_ref, end in zip(edge_refs, ends):
             edge_ref[row] = end
+        for i, main_ref, side_refs in (
+            (row, near_ref, near_edge_refs),
+            (clon - 1 - row, far_ref, far_edge_refs),
+        ):
+            if i < HALO:
+                main_ref[i, :clat] = plane
+                main_ref[i, clat:] = jnp.broadcast_to(mask, (EDGE, clat))
+                for edge_ref, end in zip(side_refs, ends):
+                    edge_ref[i] = end
 
 
 def prepare(pressure, mask, edges):
@@ -85,7 +97,8 @@
     return pl.pallas_call(
         body,
         out_shape=[f32(clon, clat, snaps), f32(clon, clat)]
-        + [f32(clon, EDGE, snaps)] * edges,
+        + [f32(HALO, clat + EDGE, snaps)] * 2
+        + [f32(clon, EDGE, snaps), f32(HALO, EDGE, snaps), f32(HALO, EDGE, snaps)] * edges,
         in_specs=[VMEM, VMEM],
         compiler_params=SMALL,
         name="prepare",
@@ -100,33 +113,6 @@
         jnp.where(has_left, left[:1], 0.0),
         jnp.where(has_right, right[EDGE - 1 :], 0.0),
     )
-
-
-def pack_kernel(turned_ref, mask_ref, left_ref, right_ref, near_ref, far_ref, *, clon, clat):
-    _, _, has_left, has_right = place()
-    zeros = jnp.zeros((EDGE - 3, clat), jnp.float32)
-    for which, out_ref in enumerate((near_ref, far_ref)):
-        for i in range(HALO):
-            row = clon - 1 - i if which else i
-            left, right, left_mask, right_mask = ends_of(left_ref, right_ref, row, has_left, has_right)
-            out_ref[i, :EDGE] = left
-            out_ref[i, EDGE : EDGE + clat] = turned_ref[row]
-            out_ref[i, EDGE + clat : 2 * EDGE + clat] = right
-            out_ref[i, 2 * EDGE + clat :] = jnp.concatenate(
-                [mask_ref[row : row + 1], left_mask, right_mask, zeros], axis=0
-            )
-
-
-def pack(turned, mask, left, right):
-    clon, clat, snaps = turned.shape
-    block = f32(HALO, clat + 3 * EDGE, snaps)
-    return pl.pallas_call(
-        functools.partial(pack_kernel, clon=clon, clat=clat),
-        out_shape=[block, block],
-        in_specs=[VMEM] * 4,
-        compiler_params=SMALL,
-        name="pack",
-    )(turned, mask, left, right)
 
 
 class Tables:
@@ -191,6 +177,14 @@
         return carry
 
     lax.fori_loop(begin, end, one, 0)
+
+
+def start_row(tables, field, row, ends, middle):
+    kept = tables.quarter[row] * 4.0
+    clat = middle.shape[0]
+    field[row, EDGE : 2 * EDGE] = ends[0] * kept[:EDGE]
+    field[row, 2 * EDGE : 2 * EDGE + clat] = middle * kept[EDGE : EDGE + clat]
+    field[row, 2 * EDGE + clat : 3 * EDGE + clat] = ends[1] * kept[EDGE + clat :]
 
 
 def clear_ends(swept, rows, tall, snaps):
@@ -268,7 +262,8 @@
 
 
 def near_kernel(
-    turned_ref, mask_ref, left_ref, right_ref, near_ref, x_ref, rim_ref, gram_ref,
+    turned_ref, mask_ref, left_ref, right_ref, near_ref, near_left_ref, near_right_ref,
+    x_ref, rim_ref, gram_ref,
     field_a, field_b, swept, masks, keep_lon, keep_lat, quarter, *, clon, clat, snaps,
 ):
     tall = clat + 2 * EDGE
@@ -277,8 +272,8 @@
     wide = clon + HALO
     backwards, _, has_left, has_right = place()
     for i in range(HALO):
-        marks = near_ref[i, tall:]
-        tables.put_masks(HALO - 1 - i, marks[0:1], marks[1:2], marks[2:3])
+        ends = ends_of(near_left_ref, near_right_ref, i, has_left, has_right)
+        tables.put_masks(HALO - 1 - i, near_ref[i, clat : clat + 1], *ends[2:])
     for row in range(clon):
         ends = ends_of(left_ref, right_ref, row, has_left, has_right)
         tables.put_masks(HALO + row, mask_ref[row : row + 1], *ends[2:])
@@ -288,19 +283,15 @@
     tables.fill(range(wide), clat)
     clear_ends(swept, range(wide), tall, snaps)
     for i in range(HALO):
-        row = HALO - 1 - i
-        field_a[row, lower:upper] = near_ref[i, :tall] * (quarter[row] * 4.0)
-
-    def start_row(row, carry):
-        here = row + HALO
-        kept = quarter[here] * 4.0
-        left, right, _, _ = ends_of(left_ref, right_ref, row, has_left, has_right)
-        field_a[here, lower : lower + EDGE] = left * kept[:EDGE]
-        field_a[here, lower + EDGE : upper - EDGE] = turned_ref[row] * kept[EDGE : EDGE + clat]
-        field_a[here, upper - EDGE : upper] = right * kept[EDGE + clat :]
+        ends = ends_of(near_left_ref, near_right_ref, i, has_left, has_right)
+        start_row(tables, field_a, HALO - 1 - i, ends, near_ref[i, :clat])
+
+    def own_row(row, carry):
+        ends = ends_of(left_ref, right_ref, row, has_left, has_right)
+        start_row(tables, field_a, row + HALO, ends, turned_ref[row])
         return carry
 
-    lax.fori_loop(0, clon, start_row, 0)
+    lax.fori_loop(0, clon, own_row, 0)
     source, target = field_a, field_b
     for step in range(PASSES + 1):
         rim_ref[step] = source[wide - 2 - step : wide - step, lower:upper]
@@ -313,7 +304,8 @@
 
 
 def far_kernel(
-    mask_ref, left_ref, right_ref, far_ref, rim_ref, gram_in_ref, x_ref, gram_ref,
+    mask_ref, left_ref, right_ref, far_ref, far_left_ref, far_right_ref, rim_ref, gram_in_ref,
+    x_ref, gram_ref,
     field_a, field_b, swept, masks, keep_lon, keep_lat, quarter, *, clon, clat, snaps,
 ):
     tall = clat + 2 * EDGE
@@ -326,16 +318,16 @@
         ends = ends_of(left_ref, right_ref, row, has_left, has_right)
         tables.put_masks(row - skip, mask_ref[row : row + 1], *ends[2:])
     for i in range(HALO):
-        marks = far_ref[i, tall:]
-        tables.put_masks(HALO + 1 + i, marks[0:1], marks[1:2], marks[2:3])
+        ends = ends_of(far_left_ref, far_right_ref, i, has_left, has_right)
+        tables.put_masks(HALO + 1 + i, far_ref[i, clat : clat + 1], *ends[2:])
     for row in range(wide, masks.shape[1]):
         zero = jnp.zeros((1, clat), jnp.float32)
         tables.put_masks(row, zero, zero, zero)
     tables.fill(range(1, wide), clat)
     clear_ends(swept, range(1, wide - 1), tall, snaps)
     for i in range(HALO):
-        row = HALO + 1 + i
-        field_a[row, lower:upper] = far_ref[i, :tall] * (quarter[row] * 4.0)
+        ends = ends_of(far_left_ref, far_right_ref, i, has_left, has_right)
+        start_row(tables, field_a, HALO + 1 + i, ends, far_ref[i, :clat])
     source, target = field_a, field_b
     for step in range(PASSES + 1):
         source[HALO - 1 - step : HALO + 1 - step, lower:upper] = rim_ref[step]
@@ -357,7 +349,7 @@
     return [field, field, field, masks, table, table, table]
 
 
-def near_part(turned, mask, left, right, near):
+def near_part(turned, mask, *halos):
     clon, clat, snaps = turned.shape
     return pl.pallas_call(
         functools.partial(near_kernel, clon=clon, clat=clat, snaps=snaps),
@@ -366,25 +358,25 @@
             f32(PASSES + 1, 2, clat + 2 * EDGE, snaps),
             f32(2, 2, snaps // 2, snaps),
         ],
-        in_specs=[VMEM] * 5,
+        in_specs=[VMEM] * 7,
         out_specs=[VMEM, VMEM, VMEM],
         scratch_shapes=filter_scratch(clon + HALO, clat, snaps),
         compiler_params=PARAMS,
         cost_estimate=pl.CostEstimate(flops=4_000_000_000, bytes_accessed=8_000_000, transcendentals=0),
         name="near_part",
-    )(turned, mask, left, right, near)
-
-
-def far_part(mask, left, right, far, rim, gram, clon, clat, snaps):
+    )(turned, mask, *halos)
+
+
+def far_part(mask, halos, rim, gram, clon, clat, snaps):
     return pl.pallas_call(
         functools.partial(far_kernel, clon=clon, clat=clat, snaps=snaps),
         out_shape=[f32(3 * HALO, snaps, clat), f32(2, 2, snaps // 2, snaps)],
-        in_specs=[VMEM] * 6,
+        in_specs=[VMEM] * 8,
         out_specs=[VMEM, VMEM],
         scratch_shapes=filter_scratch(2 * HALO + 1, clat, snaps),
         compiler_params=PARAMS,
         name="far_part",
-    )(mask, left, right, far, rim, gram)
+    )(mask, *halos, rim, gram)
 
 
 def spread(row, lane):
@@ -398,12 +390,19 @@
     lane = lax.broadcasted_iota(jnp.int32, (8, size), 1)
     sub = lax.broadcasted_iota(jnp.int32, (8, size), 0)
     uppers, inverses = [], []
+
+    def every(value, r):
+        return jnp.broadcast_to(value[r : r + 1, :], (8, size))
+
+    columns = [spread(tiles[0], c) for c in range(8)]
     for block in range(count):
         base = 8 * block
         panel = tiles[block]
         inside = (lane >= base) & (lane < base + 8)
-        rows = [jnp.broadcast_to(panel[r : r + 1, :], (8, size)) for r in range(8)]
-        entry = {(r, c): spread(rows[r], base + c) for r in range(8) for c in range(r + 1)}
+        rows = [every(panel, r) for r in range(8)]
+        entry = {(r, c): every(columns[c], r) for r in range(8) for c in range(r + 1)}
+        if block + 1 < count:
+            columns = [spread(tiles[block + 1], base + 8 + c) for c in range(8)]
         units = [jnp.where(lane == base + r, 1.0, 0.0) for r in range(8)]
         factor = {}
         pivots = []
@@ -427,6 +426,8 @@
                 for q in range(k + 1, 8):
                     raw[q] = raw[q] - scaled * entry[q, k]
                 tile = tile - scaled * joined[k]
+                if i == block + 1:
+                    columns = [columns[c] - scaled * every(raw[k], c) for c in range(8)]
             tiles[i] = tile
         upper = jnp.zeros((8, size), jnp.float32)
         inverse = jnp.zeros((8, size), jnp.float32)
@@ -598,19 +599,29 @@
     snaps, clon, clat = pressure.shape
     nlon, nlat = lax.axis_size("lon"), lax.axis_size("lat")
     merged = nlat == 2
-    turned, mask, *edges = prepare(pressure, ocean_mask.astype(jnp.float32), 1 if merged else 2)
+    turned, mask, near, far, *ends = prepare(pressure, ocean_mask.astype(jnp.float32), 1 if merged else 2)
+
+    def partner(i, side):
+        return [i, i ^ 1, (i + 1 if i % 2 else i - 1) % nlon][side]
+
+    def move(block, side, shift):
+        pairs = []
+        for i in range(nlon):
+            for j in range(nlat):
+                to = 1 - j if shift == 0 else j + shift
+                if 0 <= to < nlat:
+                    pairs.append((i * nlat + j, partner(i, side) * nlat + to))
+        return lax.ppermute(block, BOTH, pairs)
+
     if merged:
-        left = right = lax.ppermute(edges[0], "lat", [(0, 1), (1, 0)])
+        both = [move(ends[side], side, 0) for side in range(3)]
+        both = [(block, block) for block in both]
     else:
-        left = lax.ppermute(edges[1], "lat", [(i, i + 1) for i in range(nlat - 1)])
-        right = lax.ppermute(edges[0], "lat", [(i + 1, i) for i in range(nlat - 1)])
-    near, far = pack(turned, mask, left, right)
-    far = lax.ppermute(
-        far, "lon", [(i, (i + 1 if i % 2 else i - 1) % nlon) for i in range(nlon)]
-    )
-    near = lax.ppermute(near, "lon", [(i, i ^ 1) for i in range(nlon)])
-    x_near, rim, gram = near_part(turned, mask, left, right, near)
-    x_far, gram = far_part(mask, left, right, far, rim, gram, clon, clat, snaps)
+        both = [(move(ends[3 + side], side, 1), move(ends[side], side, -1)) for side in range(3)]
+    far = lax.ppermute(far, "lon", [(i, partner(i, 2)) for i in range(nlon)])
+    near = lax.ppermute(near, "lon", [(i, partner(i, 1)) for i in range(nlon)])
+    x_near, rim, gram = near_part(turned, mask, *both[0], near, *both[1])
+    x_far, gram = far_part(mask, (*both[0], far, *both[2]), rim, gram, clon, clat, snaps)
     gram = summed(gram, nlon, nlat)
     return tuple(orthonormal(gram, x_near, x_far, clon, clat, 3 * clon * clat * nlon * nlat))
 

time: 54.4 us -> 52.4 us (0.963)
  waiting for transfers between devices: 12.1 us -> 10.5 us
  Pallas kernels: 22.7 us -> 21.8 us
  starting transfers between devices: 16.4 us -> 17 us
    ppermute x3 -> x5, waiting for transfers between devices: 2.25 us -> 1.07 us  [the longest x1 1.06 us: on_device(): far = lax.ppermute(far, 'lon', [(i, partner(i, 2)) for i in range(nlon)])]
    pallas_call x1, Pallas kernels: 10.2 us -> 9.37 us  [orthonormal(): pl.pallas_call(functools.partial(modes_kernel, clon=clon, clat=clat, snap...]
    ppermute x3 -> x5, starting transfers between devices: 8.26 us -> 8.82 us  [the longest x3 8.3 us: move(): return lax.ppermute(block, BOTH, pairs)]
  transfers between devices with their start and end apart: 11 -> 13, of which waited for: 8 -> 8; matrix products, arithmetic and copies ran while one was open for 0% -> 0% of each run, Pallas kernels for 15% -> 16%
where the time goes in v2:
time: 52.4 us; the launch traced here: 52.2 us
  Pallas kernels  21.8 us (42%)
  starting transfers between devices  17 us (32%)
  waiting for transfers between devices  10.5 us (20%)
  local copies, waits for them, and re-layouts  1.22 us (2%)
  between operations  0.9 us (2%)
  other arithmetic  0.83 us (2%)
    ppermute x8, waiting for transfers between devices, partner(): return lax.ppermute(value, BOTH, [(i, i ^ step) for i in range(count)])  9.39 us
    pallas_call x1, Pallas kernels, orthonormal(): pl.pallas_call(functools.partial(modes_kernel, clon=clon, clat=clat, snap...  9.37 us
    pallas_call x1, Pallas kernels, near_part(): pl.pallas_call(functools.partial(near_kernel, clon=clon, clat=clat, snaps...  8.32 us
    ppermute x3, starting transfers between devices, move(): return lax.ppermute(block, BOTH, pairs)  8.3 us
    ppermute x8, starting transfers between devices, partner(): return lax.ppermute(value, BOTH, [(i, i ^ step) for i in range(count)])  8.14 us
    pallas_call x1, Pallas kernels, far_part(): pl.pallas_call(functools.partial(far_kernel, clon=clon, clat=clat, snaps=...  3.7 us
    unnamed x2, local copies, waits for them, and re-layouts  1.22 us
    ppermute x1, waiting for transfers between devices, on_device(): far = lax.ppermute(far, 'lon', [(i, partner(i, 2)) for i in range(nlon)])  1.06 us
  transfers between devices with their start and end apart: 13, of which 8 were waited for; matrix products, arithmetic and copies ran while one was open for 0% of the time, Pallas kernels for 16%

profile of v2, /device:TPU:0, one launch (start us, length us, event | category | flops | bytes accessed | tf_op | source)
XLA Modules:
  0.0 52.2 jit_solution(17995684332449721236)
XLA Ops:
  0.6 0.7 %convert_element_type.3.mask_ref = f32[16,128]{1,0:T(8,128)S(1)} convert(s32[16,128]{1,0:T(8,128)} %param.3) | non-fusion elementwise | flops 2048 | bytes 16384 | tf_op jit(solution)/shard_map/convert_element_type | solution.py:602
  1.3 1.2 %copy-done = f32[128,16,128]{2,1,0:T(8,128)S(1)} copy-done((f32[128,16,128]{2,1,0:T(8,128)S(1)}, f32[128,16,128]{2,1,0:T(8,128)}, u32[]{:S(2)}) %copy-start) | copy-done | bytes 1048600
  2.6 0.4 prepare.1
  2.9 0.5 collective-permute-start.3
  3.5 2.6 %collective-permute-start = (f32[16,8,128]{2,1,0:T(8,128)S(1)}, f32[16,8,128]{2,1,0:T(8,128)S(1)}, u32[]{:S(2)}, u32[]{:S(2)}) collective-permute-start(f32[16,8,128]{2,1,0:T(8,128)S(1)} %get-tuple-element.15), channel_id=1, source_target_pairs={{0,1},{1,0},{2,3},{3,2},{4,5},{5,4},{6,7},{7,6},{8,9},{9,8},{10,11... | collective-permute-start | bytes 196616 | tf_op jit(solution)/shard_map/ppermute | solution.py:614
  6.1 5.7 %collective-permute-start.2 = (f32[5,8,128]{2,1,0:T(8,128)S(1)}, f32[5,8,128]{2,1,0:T(8,128)S(1)}, u32[]{:S(2)}, u32[]{:S(2)}) collective-permute-start(f32[5,8,128]{2,1,0:T(8,128)S(1)} %get-tuple-element.17), channel_id=1, source_target_pairs={{0,31},{1,30},{2,5},{3,4},{4,3},{5,2},{6,9},{7,8},{8,7},{9,6},{10,... | collective-permute-start | bytes 61448 | tf_op jit(solution)/shard_map/ppermute | solution.py:614
  11.8 8.3 %near_part.1 = (f32[33,128,128]{2,1,0:T(8,128)S(1)}, f32[5,2,144,128]{3,2,1,0:T(8,128)S(1)}, f32[2,2,64,128]{3,2,1,0:T(8,128)S(1)}) custom-call(f32[16,128,128]{2,1,0:T(8,128)S(1)} %get-tuple-element.18.turned_ref, f32[16,128]{1,0:T(8,128)S(1)} %get-tuple-element.14.mask_ref, f32[16,8,128]{2,1,0:T(8,128)S(1)} %collective-permute-done.left_ref.right_ref, ...), custom_call_target="tpu_custom_call" | custom-call | flops 4000000000 | bytes 8000000 | tf_op jit(solution)/shard_map/near_part/pallas_call | solution.py:354
  20.1 1.1 %collective-permute-done.1.far_ref = f32[5,136,128]{2,1,0:T(8,128)S(1)} collective-permute-done((f32[5,136,128]{2,1,0:T(8,128)S(1)}, f32[5,136,128]{2,1,0:T(8,128)S(1)}, u32[]{:S(2)}, u32[]{:S(2)}) %collective-permute-start.1) | collective-permute-done | bytes 348192 | tf_op jit(solution)/shard_map/ppermute | solution.py:621
  21.2 3.7 %far_part.1 = (f32[15,128,128]{2,1,0:T(8,128)S(1)}, f32[2,2,64,128]{3,2,1,0:T(8,128)S(1)}) custom-call(f32[16,128]{1,0:T(8,128)S(1)} %get-tuple-element.14.mask_ref, f32[16,8,128]{2,1,0:T(8,128)S(1)} %collective-permute-done.left_ref.right_ref, f32[16,8,128]{2,1,0:T(8,128)S(1)} %collective-permute-done.left_ref.right_ref, ...), custom_call_target="tpu_custom_call" | custom-call | tf_op jit(solution)/shard_map/far_part/pallas_call | solution.py:371
  24.9 0.1 collective-permute-start.5
  25.0 1.2 %collective-permute-done.5 = f32[2,64,128]{2,1,0:T(8,128)S(1)} collective-permute-done((f32[2,64,128]{2,1,0:T(8,128)S(1)}, f32[2,64,128]{2,1,0:T(8,128)S(1)}, u32[]{:S(2)}, u32[]{:S(2)}) %collective-permute-start.5) | collective-permute-done | bytes 65568 | tf_op jit(solution)/shard_map/ppermute | solution.py:575
  26.3 0.1 collective-permute-start.8
  26.3 2.0 %collective-permute-start.7 = (f32[2,64,128]{2,1,0:T(8,128)S(1)}, f32[2,64,128]{2,1,0:T(8,128)S(1)}, u32[]{:S(2)}, u32[]{:S(2)}) collective-permute-start(f32[2,64,128]{2,1,0:T(8,128)S(1)} %pad_maximum_fusion), channel_id=1, source_target_pairs={{0,4},{1,5},{2,6},{3,7},{4,0},{5,1},{6,2},{7,3},{8,12},{9,13},{10,... | collective-permute-start | bytes 196616 | tf_op jit(solution)/shard_map/ppermute | solution.py:575
  28.3 1.5 %collective-permute-start.6 = (f32[2,64,128]{2,1,0:T(8,128)S(1)}, f32[2,64,128]{2,1,0:T(8,128)S(1)}, u32[]{:S(2)}, u32[]{:S(2)}) collective-permute-start(f32[2,64,128]{2,1,0:T(8,128)S(1)} %pad_maximum_fusion), channel_id=1, source_target_pairs={{0,1},{1,0},{2,3},{3,2},{4,5},{5,4},{6,7},{7,6},{8,9},{9,8},{10,11... | collective-permute-start | bytes 196616 | tf_op jit(solution)/shard_map/ppermute | solution.py:575
  29.8 2.3 %collective-permute-done.8 = f32[2,64,128]{2,1,0:T(8,128)S(1)} collective-permute-done((f32[2,64,128]{2,1,0:T(8,128)S(1)}, f32[2,64,128]{2,1,0:T(8,128)S(1)}, u32[]{:S(2)}, u32[]{:S(2)}) %collective-permute-start.8) | collective-permute-done | bytes 65568 | tf_op jit(solution)/shard_map/ppermute | solution.py:575
  32.1 0.5 collective-permute-done.6
  32.6 3.0 %collective-permute-start.11 = (f32[2,64,128]{2,1,0:T(8,128)S(1)}, f32[2,64,128]{2,1,0:T(8,128)S(1)}, u32[]{:S(2)}, u32[]{:S(2)}) collective-permute-start(f32[2,64,128]{2,1,0:T(8,128)S(1)} %pad_maximum_fusion.1), channel_id=1, source_target_pairs={{0,24},{1,25},{2,26},{3,27},{4,28},{5,29},{6,30},{7,31},{8,16},{9,... | collective-permute-start | bytes 196616 | tf_op jit(solution)/shard_map/ppermute | solution.py:575
  35.6 1.5 %collective-permute-start.9 = (f32[2,64,128]{2,1,0:T(8,128)S(1)}, f32[2,64,128]{2,1,0:T(8,128)S(1)}, u32[]{:S(2)}, u32[]{:S(2)}) collective-permute-start(f32[2,64,128]{2,1,0:T(8,128)S(1)} %pad_maximum_fusion.1), channel_id=1, source_target_pairs={{0,8},{1,9},{2,10},{3,11},{4,12},{5,13},{6,14},{7,15},{8,0},{9,1},... | collective-permute-start | bytes 196616 | tf_op jit(solution)/shard_map/ppermute | solution.py:575
  37.1 1.8 %collective-permute-done.11 = f32[2,64,128]{2,1,0:T(8,128)S(1)} collective-permute-done((f32[2,64,128]{2,1,0:T(8,128)S(1)}, f32[2,64,128]{2,1,0:T(8,128)S(1)}, u32[]{:S(2)}, u32[]{:S(2)}) %collective-permute-start.11) | collective-permute-done | bytes 65568 | tf_op jit(solution)/shard_map/ppermute | solution.py:575
  38.9 2.0 %collective-permute-done.10 = f32[2,64,128]{2,1,0:T(8,128)S(1)} collective-permute-done((f32[2,64,128]{2,1,0:T(8,128)S(1)}, f32[2,64,128]{2,1,0:T(8,128)S(1)}, u32[]{:S(2)}, u32[]{:S(2)}) %collective-permute-start.10) | collective-permute-done | bytes 65568 | tf_op jit(solution)/shard_map/ppermute | solution.py:575
  40.9 0.3 collective-permute-done.9
  41.3 0.1 collective-permute-start.12
  41.4 1.2 %collective-permute-done.12 = f32[2,64,128]{2,1,0:T(8,128)S(1)} collective-permute-done((f32[2,64,128]{2,1,0:T(8,128)S(1)}, f32[2,64,128]{2,1,0:T(8,128)S(1)}, u32[]{:S(2)}, u32[]{:S(2)}) %collective-permute-start.12) | collective-permute-done | bytes 65568 | tf_op jit(solution)/shard_map/ppermute | solution.py:575
  42.6 9.4 %orthonormal.1 = (f32[128,3,16,128]{3,2,1,0:T(8,128)}, f32[128,128]{1,0:T(8,128)}) custom-call(f32[2,2,64,128]{3,2,1,0:T(8,128)S(1)} %maximum_select_fusion.gram_ref, f32[33,128,128]{2,1,0:T(8,128)S(1)} %get-tuple-element.24.near_ref, f32[15,128,128]{2,1,0:T(8,128)S(1)} %get-tuple-element.25.far_ref), custom_call_target="tpu_custom_call" | custom-call | tf_op jit(solution)/shard_map/orthonormal/pallas_call | solution.py:554
  (17 shorter events, 0.2 us)
Async XLA Ops:
  1.3 1.2 %copy-start = (f32[128,16,128]{2,1,0:T(8,128)S(1)}, f32[128,16,128]{2,1,0:T(8,128)}, u32[]{:S(2)}) copy-start(f32[128,16,128]{2,1,0:T(8,128)} %param.2) | copy-start | bytes 3145732
  2.9 8.8 %collective-permute-start.3 = (f32[5,136,128]{2,1,0:T(8,128)S(1)}, f32[5,136,128]{2,1,0:T(8,128)S(1)}, u32[]{:S(2)}, u32[]{:S(2)}) collective-permute-start(f32[5,136,128]{2,1,0:T(8,128)S(1)} %get-tuple-element.19), channel_id=1, source_target_pairs={{0,2},{2,0},{4,6},{6,4},{8,10},{10,8},{12,14},{14,12},{16,18},{18,... | collective-permute-start | bytes 1044488 | tf_op jit(solution)/shard_map/ppermute | solution.py:622
  3.5 8.3 %collective-permute-start = (f32[16,8,128]{2,1,0:T(8,128)S(1)}, f32[16,8,128]{2,1,0:T(8,128)S(1)}, u32[]{:S(2)}, u32[]{:S(2)}) collective-permute-start(f32[16,8,128]{2,1,0:T(8,128)S(1)} %get-tuple-element.15), channel_id=1, source_target_pairs={{0,1},{1,0},{2,3},{3,2},{4,5},{5,4},{6,7},{7,6},{8,9},{9,8},{10,11... | collective-permute-start | bytes 196616 | tf_op jit(solution)/shard_map/ppermute | solution.py:614
  6.0 5.7 %collective-permute-start.4 = (f32[5,8,128]{2,1,0:T(8,128)S(1)}, f32[5,8,128]{2,1,0:T(8,128)S(1)}, u32[]{:S(2)}, u32[]{:S(2)}) collective-permute-start(f32[5,8,128]{2,1,0:T(8,128)S(1)} %get-tuple-element.20), channel_id=1, source_target_pairs={{0,3},{1,2},{2,1},{3,0},{4,7},{5,6},{6,5},{7,4},{8,11},{9,10},{10,... | collective-permute-start | bytes 61448 | tf_op jit(solution)/shard_map/ppermute | solution.py:614
  6.1 14.0 %collective-permute-start.2 = (f32[5,8,128]{2,1,0:T(8,128)S(1)}, f32[5,8,128]{2,1,0:T(8,128)S(1)}, u32[]{:S(2)}, u32[]{:S(2)}) collective-permute-start(f32[5,8,128]{2,1,0:T(8,128)S(1)} %get-tuple-element.17), channel_id=1, source_target_pairs={{0,31},{1,30},{2,5},{3,4},{4,3},{5,2},{6,9},{7,8},{8,7},{9,6},{10,... | collective-permute-start | bytes 61448 | tf_op jit(solution)/shard_map/ppermute | solution.py:614
  11.8 9.4 %collective-permute-start.1 = (f32[5,136,128]{2,1,0:T(8,128)S(1)}, f32[5,136,128]{2,1,0:T(8,128)S(1)}, u32[]{:S(2)}, u32[]{:S(2)}) collective-permute-start(f32[5,136,128]{2,1,0:T(8,128)S(1)} %get-tuple-element.16), channel_id=1, source_target_pairs={{0,30},{2,4},{4,2},{6,8},{8,6},{10,12},{12,10},{14,16},{16,14},{18... | collective-permute-start | bytes 1044488 | tf_op jit(solution)/shard_map/ppermute | solution.py:621
  24.9 1.3 %collective-permute-start.5 = (f32[2,64,128]{2,1,0:T(8,128)S(1)}, f32[2,64,128]{2,1,0:T(8,128)S(1)}, u32[]{:S(2)}, u32[]{:S(2)}) collective-permute-start(f32[2,64,128]{2,1,0:T(8,128)S(1)} %get-tuple-element.33), channel_id=1, source_target_pairs={{0,2},{1,3},{2,0},{3,1},{4,6},{5,7},{6,4},{7,5},{8,10},{9,11},{10,... | collective-permute-start | bytes 196616 | tf_op jit(solution)/shard_map/ppermute | solution.py:575
  26.3 5.8 %collective-permute-start.8 = (f32[2,64,128]{2,1,0:T(8,128)S(1)}, f32[2,64,128]{2,1,0:T(8,128)S(1)}, u32[]{:S(2)}, u32[]{:S(2)}) collective-permute-start(f32[2,64,128]{2,1,0:T(8,128)S(1)} %pad_maximum_fusion), channel_id=1, source_target_pairs={{0,5},{1,4},{2,7},{3,6},{4,1},{5,0},{6,3},{7,2},{8,13},{9,12},{10,... | collective-permute-start | bytes 196616 | tf_op jit(solution)/shard_map/ppermute | solution.py:575
  26.3 5.7 %collective-permute-start.7 = (f32[2,64,128]{2,1,0:T(8,128)S(1)}, f32[2,64,128]{2,1,0:T(8,128)S(1)}, u32[]{:S(2)}, u32[]{:S(2)}) collective-permute-start(f32[2,64,128]{2,1,0:T(8,128)S(1)} %pad_maximum_fusion), channel_id=1, source_target_pairs={{0,4},{1,5},{2,6},{3,7},{4,0},{5,1},{6,2},{7,3},{8,12},{9,13},{10,... | collective-permute-start | bytes 196616 | tf_op jit(solution)/shard_map/ppermute | solution.py:575
  28.3 4.3 %collective-permute-start.6 = (f32[2,64,128]{2,1,0:T(8,128)S(1)}, f32[2,64,128]{2,1,0:T(8,128)S(1)}, u32[]{:S(2)}, u32[]{:S(2)}) collective-permute-start(f32[2,64,128]{2,1,0:T(8,128)S(1)} %pad_maximum_fusion), channel_id=1, source_target_pairs={{0,1},{1,0},{2,3},{3,2},{4,5},{5,4},{6,7},{7,6},{8,9},{9,8},{10,11... | collective-permute-start | bytes 196616 | tf_op jit(solution)/shard_map/ppermute | solution.py:575
  32.6 6.3 %collective-permute-start.11 = (f32[2,64,128]{2,1,0:T(8,128)S(1)}, f32[2,64,128]{2,1,0:T(8,128)S(1)}, u32[]{:S(2)}, u32[]{:S(2)}) collective-permute-start(f32[2,64,128]{2,1,0:T(8,128)S(1)} %pad_maximum_fusion.1), channel_id=1, source_target_pairs={{0,24},{1,25},{2,26},{3,27},{4,28},{5,29},{6,30},{7,31},{8,16},{9,... | collective-permute-start | bytes 196616 | tf_op jit(solution)/shard_map/ppermute | solution.py:575
  35.6 5.3 %collective-permute-start.10 = (f32[2,64,128]{2,1,0:T(8,128)S(1)}, f32[2,64,128]{2,1,0:T(8,128)S(1)}, u32[]{:S(2)}, u32[]{:S(2)}) collective-permute-start(f32[2,64,128]{2,1,0:T(8,128)S(1)} %pad_maximum_fusion.1), channel_id=1, source_target_pairs={{0,16},{1,17},{2,18},{3,19},{4,20},{5,21},{6,22},{7,23},{8,24},{9,... | collective-permute-start | bytes 196616 | tf_op jit(solution)/shard_map/ppermute | solution.py:575
  35.6 5.6 %collective-permute-start.9 = (f32[2,64,128]{2,1,0:T(8,128)S(1)}, f32[2,64,128]{2,1,0:T(8,128)S(1)}, u32[]{:S(2)}, u32[]{:S(2)}) collective-permute-start(f32[2,64,128]{2,1,0:T(8,128)S(1)} %pad_maximum_fusion.1), channel_id=1, source_target_pairs={{0,8},{1,9},{2,10},{3,11},{4,12},{5,13},{6,14},{7,15},{8,0},{9,1},... | collective-permute-start | bytes 196616 | tf_op jit(solution)/shard_map/ppermute | solution.py:575
  41.3 1.3 %collective-permute-start.12 = (f32[2,64,128]{2,1,0:T(8,128)S(1)}, f32[2,64,128]{2,1,0:T(8,128)S(1)}, u32[]{:S(2)}, u32[]{:S(2)}) collective-permute-start(f32[2,64,128]{2,1,0:T(8,128)S(1)} %get-tuple-element.35), channel_id=1, source_target_pairs={{0,2},{1,3},{2,0},{3,1},{4,6},{5,7},{6,4},{7,5},{8,10},{9,11},{10,... | collective-permute-start | bytes 196616 | tf_op jit(solution)/shard_map/ppermute | solution.py:575

commit v3 on v2

--- a/solution.py
+++ b/solution.py
@@ -10,6 +10,7 @@
 PASSES = 4
 HALO = PASSES + 1
 EDGE = 8
+DEPTH = 4
 NEAR_ONE = 2.0**-6
 ROUND = 1.5 * 2.0**23
 BOTH = ("lon", "lat")
@@ -52,27 +53,42 @@
 
 def slices_of(scaled):
     first = (scaled + ROUND) - ROUND
-    rest = (scaled - first) * 256.0
-    second = (rest + ROUND) - ROUND
-    rest = (rest - second) * 256.0
-    third = (rest + ROUND) - ROUND
-    return first, second, third
+    rest = scaled - first
+    second = (rest + ROUND * 2.0**-8) - ROUND * 2.0**-8
+    return first, second, rest - second
 
 
 def longitude(backwards, row, clon):
     return row + backwards * (clon - 1 - 2 * row)
 
 
+def plane_of(pressure_ref, mask_ref, row, clon, snaps):
+    spot = longitude(place()[0], row, clon)
+    return pressure_ref[pl.ds(spot, snaps, stride=clon), :].T, mask_ref[pl.ds(spot, 1), :]
+
+
+def far_rows_kernel(pressure_ref, mask_ref, far_ref, *, clon, clat, snaps):
+    masks = []
+    for i in range(HALO):
+        plane, mask = plane_of(pressure_ref, mask_ref, clon - 1 - i, clon, snaps)
+        far_ref[i * clat : (i + 1) * clat] = plane
+        masks.append(mask)
+    far_ref[HALO * clat :] = jnp.concatenate(masks + [jnp.zeros((EDGE - HALO, clat), jnp.float32)], axis=0)
+
+
 def prepare_kernel(
-    pressure_ref, mask_ref, turned_ref, mask_out_ref, near_ref, far_ref, *end_refs, clon, clat, snaps
+    pressure_ref, mask_ref, far_ref, turned_ref, mask_out_ref, near_ref, *end_refs, clon, clat, snaps
 ):
     edge_refs, near_edge_refs, far_edge_refs = [end_refs[i::3] for i in range(3)]
-    backwards, lat, _, _ = place()
+    lat = place()[1]
     line = lax.broadcasted_iota(jnp.int32, (EDGE, clat), 0)
     for row in range(clon):
-        spot = longitude(backwards, row, clon)
-        plane = pressure_ref[pl.ds(spot, snaps, stride=clon), :].T
-        mask = mask_ref[pl.ds(spot, 1), :]
+        if row < clon - HALO:
+            plane, mask = plane_of(pressure_ref, mask_ref, row, clon, snaps)
+        else:
+            i = clon - 1 - row
+            plane = far_ref[i * clat : (i + 1) * clat]
+            mask = far_ref[HALO * clat + i : HALO * clat + i + 1]
         turned_ref[row] = plane
         mask_out_ref[row : row + 1] = mask
         low = jnp.where(line < HALO, plane[:EDGE], mask)
@@ -80,29 +96,36 @@
         ends = (low, high) if len(edge_refs) == 2 else (jnp.where(lat == 0, high, low),)
         for edge_ref, end in zip(edge_refs, ends):
             edge_ref[row] = end
-        for i, main_ref, side_refs in (
-            (row, near_ref, near_edge_refs),
-            (clon - 1 - row, far_ref, far_edge_refs),
-        ):
+        for i, side_refs in ((row, near_edge_refs), (clon - 1 - row, far_edge_refs)):
             if i < HALO:
-                main_ref[i, :clat] = plane
-                main_ref[i, clat:] = jnp.broadcast_to(mask, (EDGE, clat))
                 for edge_ref, end in zip(side_refs, ends):
                     edge_ref[i] = end
+        if row < HALO:
+            near_ref[row * clat : (row + 1) * clat] = plane
+            near_ref[HALO * clat + row : HALO * clat + row + 1] = mask
 
 
 def prepare(pressure, mask, edges):
     snaps, clon, clat = pressure.shape
-    body = functools.partial(prepare_kernel, clon=clon, clat=clat, snaps=snaps)
-    return pl.pallas_call(
-        body,
-        out_shape=[f32(clon, clat, snaps), f32(clon, clat)]
-        + [f32(HALO, clat + EDGE, snaps)] * 2
-        + [f32(clon, EDGE, snaps), f32(HALO, EDGE, snaps), f32(HALO, EDGE, snaps)] * edges,
+    sizes = dict(clon=clon, clat=clat, snaps=snaps)
+    rows = f32(HALO * clat + EDGE, snaps)
+    inputs = (pressure.reshape(snaps * clon, clat), mask)
+    far = pl.pallas_call(
+        functools.partial(far_rows_kernel, **sizes),
+        out_shape=rows,
         in_specs=[VMEM, VMEM],
         compiler_params=SMALL,
+        name="far_rows",
+    )(*inputs)
+    turned, mask, near, *ends = pl.pallas_call(
+        functools.partial(prepare_kernel, **sizes),
+        out_shape=[f32(clon, clat, snaps), f32(clon, clat), rows]
+        + [f32(clon, EDGE, snaps), f32(HALO, EDGE, snaps), f32(HALO, EDGE, snaps)] * edges,
+        in_specs=[VMEM, VMEM, VMEM],
+        compiler_params=SMALL,
         name="prepare",
-    )(pressure.reshape(snaps * clon, clat), mask)
+    )(*inputs, far)
+    return turned, mask, near, far, ends
 
 
 def ends_of(left_ref, right_ref, row, has_left, has_right):
@@ -144,7 +167,6 @@
             return (
                 mask * (1.0 - 0.25 * across),
                 mask * (1.0 - 0.25 * (south + north)),
-                0.25 * mask,
             )
 
         middle = coefficients(
@@ -154,14 +176,15 @@
         )
         lower = coefficients(left, up(left), jnp.where(last_lane, down(own), down(left)))
         upper = coefficients(right, jnp.where(first_lane, up(own), up(right)), down(right))
-        for which, table in enumerate((self.keep_lon, self.keep_lat, self.quarter)):
+        for which, table in enumerate((self.keep_lon, self.keep_lat)):
             column = jnp.concatenate(
                 [lower[which].T[clat - EDGE :], middle[which].T, upper[which].T[:EDGE]], axis=0
             )
             for row in rows:
-                table[row] = jnp.broadcast_to(
-                    column[:, row : row + 1], (clat + 2 * EDGE, table.shape[2])
-                )
+                spread_out = jnp.broadcast_to(column[:, row : row + 1], (clat + 2 * EDGE, table.shape[2]))
+                table[row] = spread_out
+                if which == 0:
+                    self.quarter[row] = jnp.where(spread_out > 0.0, 0.25, 0.0)
 
 
 def sweep(tables, source, target, swept, begin, end, tall):
@@ -176,7 +199,7 @@
         target[row, lower:upper] = tables.keep_lat[row] * middle + near * around
         return carry
 
-    lax.fori_loop(begin, end, one, 0)
+    lax.fori_loop(begin, end, one, 0, unroll=True)
 
 
 def start_row(tables, field, row, ends, middle):
@@ -194,57 +217,56 @@
         swept[row, EDGE + tall :] = zeros
 
 
-def fields_of(backwards, tables, source, planes, rows, offset, clat, snaps):
+def fields_and_gram(backwards, tables, source, planes, rows, offset, clat, snaps):
     begin = 2 * EDGE
     end = begin + clat
     count = len(rows)
+    first = rows[0] + offset
     sign = jnp.where(backwards > 0, -2.0, 2.0)
 
-    def one(i, top):
-        here = rows[0] + i + offset
-        center = source[here, begin:end]
+    top = jnp.zeros((clat + 2 * EDGE, snaps), jnp.float32)
+    for i in range(count + 2):
+        top = jnp.maximum(top, jnp.abs(source[first - 1 + i, EDGE : end + EDGE]))
+    unit = power_of_two(jnp.maximum(jnp.max(top, axis=0, keepdims=True), 2.0**-60))
+    to_whole = jnp.broadcast_to(128.0 / unit, (clat, snaps)).T
+
+    whole = jnp.zeros((snaps, snaps), jnp.int32)
+    first_second = jnp.zeros((snaps, snaps), jnp.float32)
+    second_any = jnp.zeros((snaps, 2 * snaps), jnp.float32)
+    third_any = jnp.zeros((snaps, 2 * snaps), jnp.float32)
+    parts = []
+    for i in range(count):
+        here = first + i
         quarter = tables.quarter[here, EDGE : EDGE + clat]
         along_lon = (quarter * sign) * (source[here + 1, begin:end] - source[here - 1, begin:end])
         along_lat = (quarter * 2.0) * (
             source[here, begin + 1 : end + 1] - source[here, begin - 1 : end - 1]
         )
-        for which, value in enumerate((center, along_lon, along_lat)):
+        for which, value in enumerate((source[here, begin:end], along_lon, along_lat)):
             value = value.T
             planes[which * count + i] = value
-            top = jnp.maximum(top, jnp.abs(value))
-        return top
-
-    return lax.fori_loop(0, count, one, jnp.zeros((snaps, clat), jnp.float32))
-
-
-def gram_of(planes, count, top, snaps, clat):
-    unit = power_of_two(jnp.maximum(jnp.max(top, axis=1, keepdims=True), 2.0**-60))
-    to_whole = jnp.broadcast_to(128.0 / unit, (snaps, clat))
-    whole = jnp.zeros((snaps, snaps), jnp.int32)
-    first_second = jnp.zeros((snaps, snaps), jnp.float32)
-    second_any = jnp.zeros((snaps, 2 * snaps), jnp.float32)
-    third_any = jnp.zeros((snaps, 2 * snaps), jnp.float32)
-    for begin in range(0, count, 2):
-        parts = [slices_of(planes[which] * to_whole) for which in range(begin, min(begin + 2, count))]
-        a, b, c = [
-            jnp.concatenate([piece.astype(jnp.bfloat16) for piece in same], axis=1) for same in zip(*parts)
-        ]
-        from_first = dot_nt(a, jnp.concatenate([a, b], axis=0))
-        whole = whole + from_first[:, :snaps].astype(jnp.int32)
-        first_second = first_second + from_first[:, snaps:]
-        second_any = second_any + dot_nt(b, jnp.concatenate([b, c], axis=0))
-        third_any = third_any + dot_nt(c, jnp.concatenate([a, c], axis=0))
+            parts.append([piece.astype(jnp.bfloat16) for piece in slices_of(value * to_whole)])
+            if len(parts) < DEPTH and not (i == count - 1 and which == 2):
+                continue
+            a, b, c = [jnp.concatenate(same, axis=1) for same in zip(*parts)]
+            parts = []
+            from_first = dot_nt(a, jnp.concatenate([a, b], axis=0))
+            whole = whole + from_first[:, :snaps].astype(jnp.int32)
+            first_second = first_second + from_first[:, snaps:]
+            second_any = second_any + dot_nt(b, jnp.concatenate([b, c], axis=0))
+            third_any = third_any + dot_nt(c, jnp.concatenate([a, c], axis=0))
     fine = (
         first_second
-        + (second_any[:, :snaps] * 2.0**-9 + second_any[:, snaps:] * 2.0**-16)
-        + (third_any[:, :snaps] * 2.0**-8 + third_any[:, snaps:] * 2.0**-25)
+        + (second_any[:, :snaps] * 0.5 + second_any[:, snaps:])
+        + (third_any[:, :snaps] + third_any[:, snaps:] * 0.5)
     )
     head = whole.astype(jnp.float32)
-    tail = (whole - head.astype(jnp.int32)).astype(jnp.float32) + (fine + fine.T) * 2.0**-8
+    tail = (whole - head.astype(jnp.int32)).astype(jnp.float32) + (fine + fine.T)
     total = head + tail
     tail = tail - (total - head)
     unit = jnp.broadcast_to(unit * (1.0 / 128.0), (snaps, snaps))
-    return total * unit * unit.T, tail * unit * unit.T
+    scale = unit * unit.T
+    return total * scale, tail * scale
 
 
 def add_pairs(left, right):
@@ -273,7 +295,7 @@
     backwards, _, has_left, has_right = place()
     for i in range(HALO):
         ends = ends_of(near_left_ref, near_right_ref, i, has_left, has_right)
-        tables.put_masks(HALO - 1 - i, near_ref[i, clat : clat + 1], *ends[2:])
+        tables.put_masks(HALO - 1 - i, near_ref[HALO * clat + i : HALO * clat + i + 1], *ends[2:])
     for row in range(clon):
         ends = ends_of(left_ref, right_ref, row, has_left, has_right)
         tables.put_masks(HALO + row, mask_ref[row : row + 1], *ends[2:])
@@ -284,7 +306,7 @@
     clear_ends(swept, range(wide), tall, snaps)
     for i in range(HALO):
         ends = ends_of(near_left_ref, near_right_ref, i, has_left, has_right)
-        start_row(tables, field_a, HALO - 1 - i, ends, near_ref[i, :clat])
+        start_row(tables, field_a, HALO - 1 - i, ends, near_ref[i * clat : (i + 1) * clat])
 
     def own_row(row, carry):
         ends = ends_of(left_ref, right_ref, row, has_left, has_right)
@@ -299,8 +321,7 @@
             sweep(tables, source, target, swept, step + 1, wide - 1 - step, tall)
             source, target = target, source
     rows = range(clon - HALO)
-    top = fields_of(backwards, tables, source, x_ref, rows, HALO, clat, snaps)
-    put_gram(gram_ref, *gram_of(x_ref, 3 * len(rows), top, snaps, clat))
+    put_gram(gram_ref, *fields_and_gram(backwards, tables, source, x_ref, rows, HALO, clat, snaps))
 
 
 def far_kernel(
@@ -319,7 +340,7 @@
         tables.put_masks(row - skip, mask_ref[row : row + 1], *ends[2:])
     for i in range(HALO):
         ends = ends_of(far_left_ref, far_right_ref, i, has_left, has_right)
-        tables.put_masks(HALO + 1 + i, far_ref[i, clat : clat + 1], *ends[2:])
+        tables.put_masks(HALO + 1 + i, far_ref[HALO * clat + i : HALO * clat + i + 1], *ends[2:])
     for row in range(wide, masks.shape[1]):
         zero = jnp.zeros((1, clat), jnp.float32)
         tables.put_masks(row, zero, zero, zero)
@@ -327,7 +348,7 @@
     clear_ends(swept, range(1, wide - 1), tall, snaps)
     for i in range(HALO):
         ends = ends_of(far_left_ref, far_right_ref, i, has_left, has_right)
-        start_row(tables, field_a, HALO + 1 + i, ends, far_ref[i, :clat])
+        start_row(tables, field_a, HALO + 1 + i, ends, far_ref[i * clat : (i + 1) * clat])
     source, target = field_a, field_b
     for step in range(PASSES + 1):
         source[HALO - 1 - step : HALO + 1 - step, lower:upper] = rim_ref[step]
@@ -335,8 +356,7 @@
             sweep(tables, source, target, swept, HALO - step, 2 * HALO - step, tall)
             source, target = target, source
     rows = range(clon - HALO, clon)
-    top = fields_of(backwards, tables, source, x_ref, rows, -skip, clat, snaps)
-    gram = gram_of(x_ref, 3 * len(rows), top, snaps, clat)
+    gram = fields_and_gram(backwards, tables, source, x_ref, rows, -skip, clat, snaps)
     before = [jnp.concatenate([gram_in_ref[0, part], gram_in_ref[1, part]], axis=0) for part in range(2)]
     put_gram(gram_ref, *add_pairs(before, gram))
 
@@ -469,14 +489,12 @@
     c = third.astype(jnp.bfloat16)
     exact = dot_nt(a, a)
     mixed = dot_nt(a, b)
-    mixed_small = (
-        dot_nt(a, c) + dot_nt(b, b) * 0.5 + dot_nt(b, c) * 2.0**-8 + dot_nt(c, c) * 2.0**-17
-    )
+    mixed_small = dot_nt(a, c) + dot_nt(b, b) * 0.5 + dot_nt(b, c) + dot_nt(c, c) * 0.5
     mixed = mixed + mixed.T
     mixed_small = mixed_small + mixed_small.T
-    missing = (head - exact * 2.0**-14) - mixed * 2.0**-22
-    missing = missing - mixed_small * 2.0**-30 + tail
-    lower_one = (first + second * 2.0**-8 + third * 2.0**-16) * (1.0 / 128.0)
+    missing = (head - exact * 2.0**-14) - mixed * 2.0**-14
+    missing = missing - mixed_small * 2.0**-14 + tail
+    lower_one = (first + second + c.astype(jnp.float32)) * (1.0 / 128.0)
 
     near_one = dot_nn(inverse_one, lower_one, HIGHEST)
     left_over = dot_nn(dot_nn(inverse_one, missing, HIGHEST), inverse_one.T, HIGHEST)
@@ -599,7 +617,7 @@
     snaps, clon, clat = pressure.shape
     nlon, nlat = lax.axis_size("lon"), lax.axis_size("lat")
     merged = nlat == 2
-    turned, mask, near, far, *ends = prepare(pressure, ocean_mask.astype(jnp.float32), 1 if merged else 2)
+    turned, mask, near, far, ends = prepare(pressure, ocean_mask.astype(jnp.float32), 1 if merged else 2)
 
     def partner(i, side):
         return [i, i ^ 1, (i + 1 if i % 2 else i - 1) % nlon][side]

time: 52.4 us -> 48.5 us (0.926)
  Pallas kernels: 21.8 us -> 17.9 us
    ppermute x1, starting transfers between devices: 0.01 us -> 4.74 us  [on_device(): far = lax.ppermute(far, 'lon', [(i, partner(i, 2)) for i in range(nlon)])]
    ppermute x3, starting transfers between devices: 8.3 us -> 3.57 us  [move(): return lax.ppermute(block, BOTH, pairs)]
    pallas_call x1, Pallas kernels: 8.32 us -> 5.67 us  [near_part(): pl.pallas_call(functools.partial(near_kernel, clon=clon, clat=clat, snaps...]
    pallas_call x1, Pallas kernels: 3.7 us -> 2.3 us  [far_part(): pl.pallas_call(functools.partial(far_kernel, clon=clon, clat=clat, snaps=...]
    ppermute x1, waiting for transfers between devices: 1.06 us -> 0.01 us  [on_device(): far = lax.ppermute(far, 'lon', [(i, partner(i, 2)) for i in range(nlon)])]
    ppermute x8, waiting for transfers between devices: 9.39 us -> 10.3 us  [partner(): return lax.ppermute(value, BOTH, [(i, i ^ step) for i in range(count)])]
  transfers between devices with their start and end apart: 13 -> 13, of which waited for: 8 -> 8; matrix products, arithmetic and copies ran while one was open for 0% -> 0% of each run, Pallas kernels for 16% -> 12%
where the time goes in v3:
time: 48.5 us; the launch traced here: 48.3 us
  Pallas kernels  17.9 us (37%)
  starting transfers between devices  17 us (35%)
  waiting for transfers between devices  10.5 us (22%)
  local copies, waits for them, and re-layouts  1.22 us (3%)
  between operations  0.9 us (2%)
  other arithmetic  0.83 us (2%)
    ppermute x8, waiting for transfers between devices, partner(): return lax.ppermute(value, BOTH, [(i, i ^ step) for i in range(count)])  10.3 us
    pallas_call x1, Pallas kernels, orthonormal(): pl.pallas_call(functools.partial(modes_kernel, clon=clon, clat=clat, snap...  9.4 us
    ppermute x8, starting transfers between devices, partner(): return lax.ppermute(value, BOTH, [(i, i ^ step) for i in range(count)])  8.15 us
    pallas_call x1, Pallas kernels, near_part(): pl.pallas_call(functools.partial(near_kernel, clon=clon, clat=clat, snaps...  5.67 us
    ppermute x1, starting transfers between devices, on_device(): far = lax.ppermute(far, 'lon', [(i, partner(i, 2)) for i in range(nlon)])  4.74 us
    ppermute x3, starting transfers between devices, move(): return lax.ppermute(block, BOTH, pairs)  3.57 us
    pallas_call x1, Pallas kernels, far_part(): pl.pallas_call(functools.partial(far_kernel, clon=clon, clat=clat, snaps=...  2.3 us
    unnamed x2, local copies, waits for them, and re-layouts  1.22 us
  transfers between devices with their start and end apart: 13, of which 8 were waited for; matrix products, arithmetic and copies ran while one was open for 0% of the time, Pallas kernels for 12%

profile of v3, /device:TPU:0, one launch (start us, length us, event | category | flops | bytes accessed | tf_op | source)
XLA Modules:
  0.0 48.3 jit_solution(795580833425676285)
XLA Ops:
  0.6 0.7 %convert_element_type.3.mask_ref = f32[16,128]{1,0:T(8,128)S(1)} convert(s32[16,128]{1,0:T(8,128)} %param.3) | non-fusion elementwise | flops 2048 | bytes 16384 | tf_op jit(solution)/shard_map/convert_element_type | solution.py:620
  1.3 1.2 %copy-done = f32[128,16,128]{2,1,0:T(8,128)S(1)} copy-done((f32[128,16,128]{2,1,0:T(8,128)S(1)}, f32[128,16,128]{2,1,0:T(8,128)}, u32[]{:S(2)}) %copy-start) | copy-done | bytes 1048600
  2.6 0.2 far_rows.1.far_ref
  2.7 0.3 prepare.1
  3.1 0.5 %collective-permute-start.3 = (f32[648,128]{1,0:T(8,128)S(1)}, f32[648,128]{1,0:T(8,128)S(1)}, u32[]{:S(2)}, u32[]{:S(2)}) collective-permute-start(f32[648,128]{1,0:T(8,128)S(1)} %get-tuple-element.17), channel_id=1, source_target_pairs={{0,2},{2,0},{4,6},{6,4},{8,10},{10,8},{12,14},{14,12},{16,18},{18,... | collective-permute-start | bytes 995336 | tf_op jit(solution)/shard_map/ppermute | solution.py:640
  3.6 2.6 %collective-permute-start = (f32[16,8,128]{2,1,0:T(8,128)S(1)}, f32[16,8,128]{2,1,0:T(8,128)S(1)}, u32[]{:S(2)}, u32[]{:S(2)}) collective-permute-start(f32[16,8,128]{2,1,0:T(8,128)S(1)} %get-tuple-element.14), channel_id=1, source_target_pairs={{0,1},{1,0},{2,3},{3,2},{4,5},{5,4},{6,7},{7,6},{8,9},{9,8},{10,11... | collective-permute-start | bytes 196616 | tf_op jit(solution)/shard_map/ppermute | solution.py:632
  6.2 4.7 %collective-permute-start.1 = (f32[648,128]{1,0:T(8,128)S(1)}, f32[648,128]{1,0:T(8,128)S(1)}, u32[]{:S(2)}, u32[]{:S(2)}) collective-permute-start(f32[648,128]{1,0:T(8,128)S(1)} %far_rows.1.far_ref), channel_id=1, source_target_pairs={{0,30},{2,4},{4,2},{6,8},{8,6},{10,12},{12,10},{14,16},{16,14},{18... | collective-permute-start | bytes 995336 | tf_op jit(solution)/shard_map/ppermute | solution.py:639
  11.0 0.9 %collective-permute-start.2 = (f32[5,8,128]{2,1,0:T(8,128)S(1)}, f32[5,8,128]{2,1,0:T(8,128)S(1)}, u32[]{:S(2)}, u32[]{:S(2)}) collective-permute-start(f32[5,8,128]{2,1,0:T(8,128)S(1)} %get-tuple-element.15), channel_id=1, source_target_pairs={{0,31},{1,30},{2,5},{3,4},{4,3},{5,2},{6,9},{7,8},{8,7},{9,6},{10,... | collective-permute-start | bytes 61448 | tf_op jit(solution)/shard_map/ppermute | solution.py:632
  11.9 5.7 %near_part.1 = (f32[33,128,128]{2,1,0:T(8,128)S(1)}, f32[5,2,144,128]{3,2,1,0:T(8,128)S(1)}, f32[2,2,64,128]{3,2,1,0:T(8,128)S(1)}) custom-call(f32[16,128,128]{2,1,0:T(8,128)S(1)} %get-tuple-element.16.turned_ref, f32[16,128]{1,0:T(8,128)S(1)} %get-tuple-element.13.mask_ref, f32[16,8,128]{2,1,0:T(8,128)S(1)} %collective-permute-done.left_ref.right_ref, ...), custom_call_target="tpu_custom_call" | custom-call | flops 4000000000 | bytes 8000000 | tf_op jit(solution)/shard_map/near_part/pallas_call | solution.py:374
  17.6 0.2 collective-permute-done.2.far_left_ref.far_right_ref
  17.8 2.3 %far_part.1 = (f32[15,128,128]{2,1,0:T(8,128)S(1)}, f32[2,2,64,128]{3,2,1,0:T(8,128)S(1)}) custom-call(f32[16,128]{1,0:T(8,128)S(1)} %get-tuple-element.13.mask_ref, f32[16,8,128]{2,1,0:T(8,128)S(1)} %collective-permute-done.left_ref.right_ref, f32[16,8,128]{2,1,0:T(8,128)S(1)} %collective-permute-done.left_ref.right_ref, ...), custom_call_target="tpu_custom_call" | custom-call | tf_op jit(solution)/shard_map/far_part/pallas_call | solution.py:391
  20.2 1.2 %collective-permute-done.5 = f32[2,64,128]{2,1,0:T(8,128)S(1)} collective-permute-done((f32[2,64,128]{2,1,0:T(8,128)S(1)}, f32[2,64,128]{2,1,0:T(8,128)S(1)}, u32[]{:S(2)}, u32[]{:S(2)}) %collective-permute-start.5) | collective-permute-done | bytes 65568 | tf_op jit(solution)/shard_map/ppermute | solution.py:593
  21.4 1.7 %collective-permute-start.8 = (f32[2,64,128]{2,1,0:T(8,128)S(1)}, f32[2,64,128]{2,1,0:T(8,128)S(1)}, u32[]{:S(2)}, u32[]{:S(2)}) collective-permute-start(f32[2,64,128]{2,1,0:T(8,128)S(1)} %pad_maximum_fusion), channel_id=1, source_target_pairs={{0,5},{1,4},{2,7},{3,6},{4,1},{5,0},{6,3},{7,2},{8,13},{9,12},{10,... | collective-permute-start | bytes 196616 | tf_op jit(solution)/shard_map/ppermute | solution.py:593
  23.2 1.3 %collective-permute-start.7 = (f32[2,64,128]{2,1,0:T(8,128)S(1)}, f32[2,64,128]{2,1,0:T(8,128)S(1)}, u32[]{:S(2)}, u32[]{:S(2)}) collective-permute-start(f32[2,64,128]{2,1,0:T(8,128)S(1)} %pad_maximum_fusion), channel_id=1, source_target_pairs={{0,4},{1,5},{2,6},{3,7},{4,0},{5,1},{6,2},{7,3},{8,12},{9,13},{10,... | collective-permute-start | bytes 196616 | tf_op jit(solution)/shard_map/ppermute | solution.py:593
  24.5 0.5 %collective-permute-start.6 = (f32[2,64,128]{2,1,0:T(8,128)S(1)}, f32[2,64,128]{2,1,0:T(8,128)S(1)}, u32[]{:S(2)}, u32[]{:S(2)}) collective-permute-start(f32[2,64,128]{2,1,0:T(8,128)S(1)} %pad_maximum_fusion), channel_id=1, source_target_pairs={{0,1},{1,0},{2,3},{3,2},{4,5},{5,4},{6,7},{7,6},{8,9},{9,8},{10,11... | collective-permute-start | bytes 196616 | tf_op jit(solution)/shard_map/ppermute | solution.py:593
  25.0 1.7 %collective-permute-done.8 = f32[2,64,128]{2,1,0:T(8,128)S(1)} collective-permute-done((f32[2,64,128]{2,1,0:T(8,128)S(1)}, f32[2,64,128]{2,1,0:T(8,128)S(1)}, u32[]{:S(2)}, u32[]{:S(2)}) %collective-permute-start.8) | collective-permute-done | bytes 65568 | tf_op jit(solution)/shard_map/ppermute | solution.py:593
  26.7 1.2 %collective-permute-done.7 = f32[2,64,128]{2,1,0:T(8,128)S(1)} collective-permute-done((f32[2,64,128]{2,1,0:T(8,128)S(1)}, f32[2,64,128]{2,1,0:T(8,128)S(1)}, u32[]{:S(2)}, u32[]{:S(2)}) %collective-permute-start.7) | collective-permute-done | bytes 65568 | tf_op jit(solution)/shard_map/ppermute | solution.py:593
  28.0 0.8 %collective-permute-done.6 = f32[2,64,128]{2,1,0:T(8,128)S(1)} collective-permute-done((f32[2,64,128]{2,1,0:T(8,128)S(1)}, f32[2,64,128]{2,1,0:T(8,128)S(1)}, u32[]{:S(2)}, u32[]{:S(2)}) %collective-permute-start.6) | collective-permute-done | bytes 65568 | tf_op jit(solution)/shard_map/ppermute | solution.py:593
  28.8 2.9 %collective-permute-start.11 = (f32[2,64,128]{2,1,0:T(8,128)S(1)}, f32[2,64,128]{2,1,0:T(8,128)S(1)}, u32[]{:S(2)}, u32[]{:S(2)}) collective-permute-start(f32[2,64,128]{2,1,0:T(8,128)S(1)} %pad_maximum_fusion.1), channel_id=1, source_target_pairs={{0,24},{1,25},{2,26},{3,27},{4,28},{5,29},{6,30},{7,31},{8,16},{9,... | collective-permute-start | bytes 196616 | tf_op jit(solution)/shard_map/ppermute | solution.py:593
  31.7 1.5 %collective-permute-start.9 = (f32[2,64,128]{2,1,0:T(8,128)S(1)}, f32[2,64,128]{2,1,0:T(8,128)S(1)}, u32[]{:S(2)}, u32[]{:S(2)}) collective-permute-start(f32[2,64,128]{2,1,0:T(8,128)S(1)} %pad_maximum_fusion.1), channel_id=1, source_target_pairs={{0,8},{1,9},{2,10},{3,11},{4,12},{5,13},{6,14},{7,15},{8,0},{9,1},... | collective-permute-start | bytes 196616 | tf_op jit(solution)/shard_map/ppermute | solution.py:593
  33.2 1.7 %collective-permute-done.11 = f32[2,64,128]{2,1,0:T(8,128)S(1)} collective-permute-done((f32[2,64,128]{2,1,0:T(8,128)S(1)}, f32[2,64,128]{2,1,0:T(8,128)S(1)}, u32[]{:S(2)}, u32[]{:S(2)}) %collective-permute-start.11) | collective-permute-done | bytes 65568 | tf_op jit(solution)/shard_map/ppermute | solution.py:593
  34.9 2.4 %collective-permute-done.10 = f32[2,64,128]{2,1,0:T(8,128)S(1)} collective-permute-done((f32[2,64,128]{2,1,0:T(8,128)S(1)}, f32[2,64,128]{2,1,0:T(8,128)S(1)}, u32[]{:S(2)}, u32[]{:S(2)}) %collective-permute-start.10) | collective-permute-done | bytes 65568 | tf_op jit(solution)/shard_map/ppermute | solution.py:593
  37.5 1.2 %collective-permute-done.12 = f32[2,64,128]{2,1,0:T(8,128)S(1)} collective-permute-done((f32[2,64,128]{2,1,0:T(8,128)S(1)}, f32[2,64,128]{2,1,0:T(8,128)S(1)}, u32[]{:S(2)}, u32[]{:S(2)}) %collective-permute-start.12) | collective-permute-done | bytes 65568 | tf_op jit(solution)/shard_map/ppermute | solution.py:593
  38.7 9.4 %orthonormal.1 = (f32[128,3,16,128]{3,2,1,0:T(8,128)}, f32[128,128]{1,0:T(8,128)}) custom-call(f32[2,2,64,128]{3,2,1,0:T(8,128)S(1)} %maximum_select_fusion.gram_ref, f32[33,128,128]{2,1,0:T(8,128)S(1)} %get-tuple-element.22.near_ref, f32[15,128,128]{2,1,0:T(8,128)S(1)} %get-tuple-element.23.far_ref), custom_call_target="tpu_custom_call" | custom-call | tf_op jit(solution)/shard_map/orthonormal/pallas_call | solution.py:572
  (18 shorter events, 0.4 us)
Async XLA Ops:
  1.3 1.2 %copy-start = (f32[128,16,128]{2,1,0:T(8,128)S(1)}, f32[128,16,128]{2,1,0:T(8,128)}, u32[]{:S(2)}) copy-start(f32[128,16,128]{2,1,0:T(8,128)} %param.2) | copy-start | bytes 3145732
  3.1 8.8 %collective-permute-start.3 = (f32[648,128]{1,0:T(8,128)S(1)}, f32[648,128]{1,0:T(8,128)S(1)}, u32[]{:S(2)}, u32[]{:S(2)}) collective-permute-start(f32[648,128]{1,0:T(8,128)S(1)} %get-tuple-element.17), channel_id=1, source_target_pairs={{0,2},{2,0},{4,6},{6,4},{8,10},{10,8},{12,14},{14,12},{16,18},{18,... | collective-permute-start | bytes 995336 | tf_op jit(solution)/shard_map/ppermute | solution.py:640
  3.6 8.3 %collective-permute-start = (f32[16,8,128]{2,1,0:T(8,128)S(1)}, f32[16,8,128]{2,1,0:T(8,128)S(1)}, u32[]{:S(2)}, u32[]{:S(2)}) collective-permute-start(f32[16,8,128]{2,1,0:T(8,128)S(1)} %get-tuple-element.14), channel_id=1, source_target_pairs={{0,1},{1,0},{2,3},{3,2},{4,5},{5,4},{6,7},{7,6},{8,9},{9,8},{10,11... | collective-permute-start | bytes 196616 | tf_op jit(solution)/shard_map/ppermute | solution.py:632
  6.1 5.7 %collective-permute-start.4 = (f32[5,8,128]{2,1,0:T(8,128)S(1)}, f32[5,8,128]{2,1,0:T(8,128)S(1)}, u32[]{:S(2)}, u32[]{:S(2)}) collective-permute-start(f32[5,8,128]{2,1,0:T(8,128)S(1)} %get-tuple-element.18), channel_id=1, source_target_pairs={{0,3},{1,2},{2,1},{3,0},{4,7},{5,6},{6,5},{7,4},{8,11},{9,10},{10,... | collective-permute-start | bytes 61448 | tf_op jit(solution)/shard_map/ppermute | solution.py:632
  6.2 11.6 %collective-permute-start.1 = (f32[648,128]{1,0:T(8,128)S(1)}, f32[648,128]{1,0:T(8,128)S(1)}, u32[]{:S(2)}, u32[]{:S(2)}) collective-permute-start(f32[648,128]{1,0:T(8,128)S(1)} %far_rows.1.far_ref), channel_id=1, source_target_pairs={{0,30},{2,4},{4,2},{6,8},{8,6},{10,12},{12,10},{14,16},{16,14},{18... | collective-permute-start | bytes 995336 | tf_op jit(solution)/shard_map/ppermute | solution.py:639
  11.0 6.8 %collective-permute-start.2 = (f32[5,8,128]{2,1,0:T(8,128)S(1)}, f32[5,8,128]{2,1,0:T(8,128)S(1)}, u32[]{:S(2)}, u32[]{:S(2)}) collective-permute-start(f32[5,8,128]{2,1,0:T(8,128)S(1)} %get-tuple-element.15), channel_id=1, source_target_pairs={{0,31},{1,30},{2,5},{3,4},{4,3},{5,2},{6,9},{7,8},{8,7},{9,6},{10,... | collective-permute-start | bytes 61448 | tf_op jit(solution)/shard_map/ppermute | solution.py:632
  20.1 1.3 %collective-permute-start.5 = (f32[2,64,128]{2,1,0:T(8,128)S(1)}, f32[2,64,128]{2,1,0:T(8,128)S(1)}, u32[]{:S(2)}, u32[]{:S(2)}) collective-permute-start(f32[2,64,128]{2,1,0:T(8,128)S(1)} %get-tuple-element.31), channel_id=1, source_target_pairs={{0,2},{1,3},{2,0},{3,1},{4,6},{5,7},{6,4},{7,5},{8,10},{9,11},{10,... | collective-permute-start | bytes 196616 | tf_op jit(solution)/shard_map/ppermute | solution.py:593
  21.4 5.3 %collective-permute-start.8 = (f32[2,64,128]{2,1,0:T(8,128)S(1)}, f32[2,64,128]{2,1,0:T(8,128)S(1)}, u32[]{:S(2)}, u32[]{:S(2)}) collective-permute-start(f32[2,64,128]{2,1,0:T(8,128)S(1)} %pad_maximum_fusion), channel_id=1, source_target_pairs={{0,5},{1,4},{2,7},{3,6},{4,1},{5,0},{6,3},{7,2},{8,13},{9,12},{10,... | collective-permute-start | bytes 196616 | tf_op jit(solution)/shard_map/ppermute | solution.py:593
  23.2 4.8 %collective-permute-start.7 = (f32[2,64,128]{2,1,0:T(8,128)S(1)}, f32[2,64,128]{2,1,0:T(8,128)S(1)}, u32[]{:S(2)}, u32[]{:S(2)}) collective-permute-start(f32[2,64,128]{2,1,0:T(8,128)S(1)} %pad_maximum_fusion), channel_id=1, source_target_pairs={{0,4},{1,5},{2,6},{3,7},{4,0},{5,1},{6,2},{7,3},{8,12},{9,13},{10,... | collective-permute-start | bytes 196616 | tf_op jit(solution)/shard_map/ppermute | solution.py:593
  24.5 4.3 %collective-permute-start.6 = (f32[2,64,128]{2,1,0:T(8,128)S(1)}, f32[2,64,128]{2,1,0:T(8,128)S(1)}, u32[]{:S(2)}, u32[]{:S(2)}) collective-permute-start(f32[2,64,128]{2,1,0:T(8,128)S(1)} %pad_maximum_fusion), channel_id=1, source_target_pairs={{0,1},{1,0},{2,3},{3,2},{4,5},{5,4},{6,7},{7,6},{8,9},{9,8},{10,11... | collective-permute-start | bytes 196616 | tf_op jit(solution)/shard_map/ppermute | solution.py:593
  28.8 6.1 %collective-permute-start.11 = (f32[2,64,128]{2,1,0:T(8,128)S(1)}, f32[2,64,128]{2,1,0:T(8,128)S(1)}, u32[]{:S(2)}, u32[]{:S(2)}) collective-permute-start(f32[2,64,128]{2,1,0:T(8,128)S(1)} %pad_maximum_fusion.1), channel_id=1, source_target_pairs={{0,24},{1,25},{2,26},{3,27},{4,28},{5,29},{6,30},{7,31},{8,16},{9,... | collective-permute-start | bytes 196616 | tf_op jit(solution)/shard_map/ppermute | solution.py:593
  31.7 5.6 %collective-permute-start.10 = (f32[2,64,128]{2,1,0:T(8,128)S(1)}, f32[2,64,128]{2,1,0:T(8,128)S(1)}, u32[]{:S(2)}, u32[]{:S(2)}) collective-permute-start(f32[2,64,128]{2,1,0:T(8,128)S(1)} %pad_maximum_fusion.1), channel_id=1, source_target_pairs={{0,16},{1,17},{2,18},{3,19},{4,20},{5,21},{6,22},{7,23},{8,24},{9,... | collective-permute-start | bytes 196616 | tf_op jit(solution)/shard_map/ppermute | solution.py:593
  31.7 5.6 %collective-permute-start.9 = (f32[2,64,128]{2,1,0:T(8,128)S(1)}, f32[2,64,128]{2,1,0:T(8,128)S(1)}, u32[]{:S(2)}, u32[]{:S(2)}) collective-permute-start(f32[2,64,128]{2,1,0:T(8,128)S(1)} %pad_maximum_fusion.1), channel_id=1, source_target_pairs={{0,8},{1,9},{2,10},{3,11},{4,12},{5,13},{6,14},{7,15},{8,0},{9,1},... | collective-permute-start | bytes 196616 | tf_op jit(solution)/shard_map/ppermute | solution.py:593
  37.4 1.3 %collective-permute-start.12 = (f32[2,64,128]{2,1,0:T(8,128)S(1)}, f32[2,64,128]{2,1,0:T(8,128)S(1)}, u32[]{:S(2)}, u32[]{:S(2)}) collective-permute-start(f32[2,64,128]{2,1,0:T(8,128)S(1)} %get-tuple-element.33), channel_id=1, source_target_pairs={{0,2},{1,3},{2,0},{3,1},{4,6},{5,7},{6,4},{7,5},{8,10},{9,11},{10,... | collective-permute-start | bytes 196616 | tf_op jit(solution)/shard_map/ppermute | solution.py:593

commit v4 on v3

--- a/solution.py
+++ b/solution.py
@@ -468,8 +468,49 @@
     return first, second, third
 
 
+def split_kernel(near_ref, far_ref, first_ref, second_ref, third_ref, *, near_rows, far_rows):
+    rows = near_rows + far_rows
+    for which in range(3):
+        for q in range(rows):
+            if q < near_rows:
+                plane = near_ref[which * near_rows + q]
+            else:
+                plane = far_ref[which * far_rows + q - near_rows]
+            for ref, part in zip((first_ref, second_ref, third_ref), thirds(plane)):
+                ref[which * rows + q] = part
+
+
+def split(x_near, x_far):
+    count = x_near.shape[0] + x_far.shape[0]
+    part = jax.ShapeDtypeStruct((count, *x_near.shape[1:]), jnp.bfloat16)
+    body = functools.partial(split_kernel, near_rows=x_near.shape[0] // 3, far_rows=x_far.shape[0] // 3)
+    return pl.pallas_call(
+        body,
+        out_shape=[part] * 3,
+        in_specs=[VMEM] * 2,
+        compiler_params=SMALL,
+        cost_estimate=pl.CostEstimate(flops=10_000_000, bytes_accessed=2_000_000, transcendentals=0),
+        name="split",
+    )(x_near, x_far)
+
+
+def halves(value):
+    first = value.astype(jnp.bfloat16)
+    return first, (value - first.astype(jnp.float32)).astype(jnp.bfloat16)
+
+
+def dot_nn_close(left, right):
+    (a, b), (c, d) = halves(left), halves(right)
+    return dot_nn(jnp.concatenate([a, b], axis=1), jnp.concatenate([c, c], axis=0)) + dot_nn(a, d)
+
+
+def dot_nt_close(left, right):
+    (a, b), (c, d) = halves(left), halves(right)
+    return dot_nt(jnp.concatenate([a, b], axis=1), jnp.concatenate([c, c], axis=1)) + dot_nt(a, d)
+
+
 def modes_kernel(
-    gram_ref, near_ref, far_ref, modes_ref, factor_ref, out_vmem, upper_vmem, combined_vmem, out_sems, *, clon, clat, snaps, total_rows
+    gram_ref, first_ref, second_ref, third_ref, modes_ref, factor_ref, out_vmem, upper_vmem, combined_vmem, out_sems, *, clon, clat, snaps, total_rows
 ):
     head, tail = [jnp.concatenate([gram_ref[0, part], gram_ref[1, part]], axis=0) for part in range(2)]
     row = lax.broadcasted_iota(jnp.int32, (snaps, snaps), 0)
@@ -496,11 +537,10 @@
     missing = missing - mixed_small * 2.0**-14 + tail
     lower_one = (first + second + c.astype(jnp.float32)) * (1.0 / 128.0)
 
-    near_one = dot_nn(inverse_one, lower_one, HIGHEST)
-    left_over = dot_nn(dot_nn(inverse_one, missing, HIGHEST), inverse_one.T, HIGHEST)
-    gram_two = dot_nn(near_one, near_one.T, HIGHEST) + left_over
-    gram_two = 0.5 * (gram_two + gram_two.T)
-    difference = gram_two - jnp.where(row == col, 1.0, 0.0)
+    one = jnp.where(row == col, 1.0, 0.0)
+    off = dot_nn(inverse_one, lower_one, HIGHEST) - one
+    left_over = dot_nt_close(dot_nn_close(inverse_one, missing), inverse_one)
+    difference = (off + off.T) + (dot_nt_close(off, off) + left_over)
 
     def lower_half(matrix):
         return jnp.where(row > col, matrix, jnp.where(row == col, 0.5 * matrix, 0.0))
@@ -516,12 +556,12 @@
         rough = k.astype(jnp.bfloat16)
         square = dot_nn(rough, rough)
         change = k - dot_nn(rough, (k - square).astype(jnp.bfloat16))
-        upper_vmem[...] = k.T + jnp.where(row == col, 1.0, 0.0)
-        combined_vmem[...] = inverse_one - dot_nn(change, inverse_one, HIGHEST)
+        upper_vmem[...] = k.T + one
+        combined_vmem[...] = inverse_one - dot_nn_close(change, inverse_one)
 
     @pl.when(jnp.logical_not(small))
     def _():
-        upper, inverse = eliminate(gram_two)
+        upper, inverse = eliminate(0.5 * (difference + difference.T) + one)
         upper_vmem[...] = upper
         combined_vmem[...] = dot_nn(inverse, inverse_one, HIGHEST)
 
@@ -531,12 +571,9 @@
     first_second = jnp.concatenate([first, second], axis=1)
     first_third = jnp.concatenate([first, third], axis=1)
     backwards, _, _, _ = place()
-    near_rows = clon - HALO
-
-    def plane(which, q):
-        if q < near_rows:
-            return near_ref[which * near_rows + q]
-        return far_ref[which * HALO + q - near_rows]
+
+    def pair(ref, plane):
+        return jnp.concatenate([ref[plane], ref[plane + 1]], axis=1)
 
     copies = []
     for which in range(3):
@@ -544,9 +581,8 @@
             spot = which * (clon // 8) + part
             flat = out_vmem.at[spot].reshape(snaps * 8, clat)
             for lon in range(0, 8, 2):
-                q = part * 8 + lon
-                both = jnp.concatenate([plane(which, q), plane(which, q + 1)], axis=1)
-                x_one, x_two, x_three = thirds(both)
+                plane = which * clon + part * 8 + lon
+                x_one, x_two, x_three = [pair(ref, plane) for ref in (first_ref, second_ref, third_ref)]
                 value = (
                     dot_nn(first_third, jnp.concatenate([x_three, x_one], axis=0))
                     + dot_nn(first_second, jnp.concatenate([x_two, x_two], axis=0))
@@ -560,19 +596,22 @@
             )
             copy.start()
             copies.append(copy)
-    factor = dot_nn(upper_vmem[...], lower_one.T, HIGHEST) * jnp.broadcast_to(grow, (snaps, snaps)).T
+    lower_two = upper_vmem[...].T
+    step = dot_nn_close(off, lower_two)
+    lower_two = lower_two - (step - dot_nn_close(off, step))
+    factor = dot_nn(lower_two.T, lower_one.T, HIGHEST) * jnp.broadcast_to(grow, (snaps, snaps)).T
     factor_ref[...] = jnp.where(col >= row, factor * (1.0 / scale), 0.0)
     for copy in copies:
         copy.wait()
 
 
-def orthonormal(gram, x_near, x_far, clon, clat, total_rows):
+def orthonormal(gram, x_parts, clon, clat, total_rows):
     snaps = gram.shape[3]
     parts = 3 * clon // 8
     return pl.pallas_call(
         functools.partial(modes_kernel, clon=clon, clat=clat, snaps=snaps, total_rows=total_rows),
         out_shape=[f32(snaps, 3, clon, clat), f32(snaps, snaps)],
-        in_specs=[VMEM] * 3,
+        in_specs=[VMEM] * 4,
         out_specs=[ANYWHERE, VMEM],
         scratch_shapes=[
             pltpu.VMEM((parts, snaps, 8, clat), jnp.float32),
@@ -582,7 +621,7 @@
         ],
         compiler_params=PARAMS,
         name="orthonormal",
-    )(gram, x_near, x_far)
+    )(gram, *x_parts)
 
 
 def summed(halves, nlon, nlat):
@@ -640,8 +679,9 @@
     near = lax.ppermute(near, "lon", [(i, partner(i, 1)) for i in range(nlon)])
     x_near, rim, gram = near_part(turned, mask, *both[0], near, *both[1])
     x_far, gram = far_part(mask, (*both[0], far, *both[2]), rim, gram, clon, clat, snaps)
+    x_parts = split(x_near, x_far)
     gram = summed(gram, nlon, nlat)
-    return tuple(orthonormal(gram, x_near, x_far, clon, clat, 3 * clon * clat * nlon * nlat))
+    return tuple(orthonormal(gram, x_parts, clon, clat, 3 * clon * clat * nlon * nlat))
 
 
 def solution(mesh):

time: 48.5 us -> 47.7 us (0.984)
  waiting for transfers between devices: 10.5 us -> 9.93 us
    pallas_call x1, Pallas kernels: 9.4 us -> 8.62 us  [orthonormal(): pl.pallas_call(functools.partial(modes_kernel, clon=clon, clat=clat, snap...]
    ppermute x8, waiting for transfers between devices: 10.3 us -> 9.74 us  [partner(): return lax.ppermute(value, BOTH, [(i, i ^ step) for i in range(count)])]
    pallas_call x0 -> x1, Pallas kernels: none -> 0.56 us  [split(): pl.pallas_call(body, out_shape=[part] * 3, in_specs=[VMEM] * 2, compiler_...]
  transfers between devices with their start and end apart: 13 -> 13, of which waited for: 8 -> 8; matrix products, arithmetic and copies ran while one was open for 0% -> 0% of each run, Pallas kernels for 12% -> 13%
where the time goes in v4:
time: 47.7 us; the launch traced here: 47.5 us
  Pallas kernels  17.7 us (37%)
  starting transfers between devices  17 us (36%)
  waiting for transfers between devices  9.93 us (21%)
  local copies, waits for them, and re-layouts  1.22 us (3%)
  between operations  0.9 us (2%)
  other arithmetic  0.83 us (2%)
    ppermute x8, waiting for transfers between devices, partner(): return lax.ppermute(value, BOTH, [(i, i ^ step) for i in range(count)])  9.74 us
    pallas_call x1, Pallas kernels, orthonormal(): pl.pallas_call(functools.partial(modes_kernel, clon=clon, clat=clat, snap...  8.62 us
    ppermute x8, starting transfers between devices, partner(): return lax.ppermute(value, BOTH, [(i, i ^ step) for i in range(count)])  8.15 us
    pallas_call x1, Pallas kernels, near_part(): pl.pallas_call(functools.partial(near_kernel, clon=clon, clat=clat, snaps...  5.67 us
    ppermute x1, starting transfers between devices, on_device(): far = lax.ppermute(far, 'lon', [(i, partner(i, 2)) for i in range(nlon)])  4.74 us
    ppermute x3, starting transfers between devices, move(): return lax.ppermute(block, BOTH, pairs)  3.57 us
    pallas_call x1, Pallas kernels, far_part(): pl.pallas_call(functools.partial(far_kernel, clon=clon, clat=clat, snaps=...  2.3 us
    unnamed x2, local copies, waits for them, and re-layouts  1.22 us
  transfers between devices with their start and end apart: 13, of which 8 were waited for; matrix products, arithmetic and copies ran while one was open for 0% of the time, Pallas kernels for 13%

profile of v4, /device:TPU:0, one launch (start us, length us, event | category | flops | bytes accessed | tf_op | source)
XLA Modules:
  0.0 47.5 jit_solution(2315490103436469367)
XLA Ops:
  0.6 0.7 %convert_element_type.3.mask_ref = f32[16,128]{1,0:T(8,128)S(1)} convert(s32[16,128]{1,0:T(8,128)} %param.3) | non-fusion elementwise | flops 2048 | bytes 16384 | tf_op jit(solution)/shard_map/convert_element_type | solution.py:659
  1.3 1.2 %copy-done = f32[128,16,128]{2,1,0:T(8,128)S(1)} copy-done((f32[128,16,128]{2,1,0:T(8,128)S(1)}, f32[128,16,128]{2,1,0:T(8,128)}, u32[]{:S(2)}) %copy-start) | copy-done | bytes 1048600
  2.7 0.3 prepare.1
  3.1 0.5 %collective-permute-start.3 = (f32[648,128]{1,0:T(8,128)S(1)}, f32[648,128]{1,0:T(8,128)S(1)}, u32[]{:S(2)}, u32[]{:S(2)}) collective-permute-start(f32[648,128]{1,0:T(8,128)S(1)} %get-tuple-element.20), channel_id=1, source_target_pairs={{0,2},{2,0},{4,6},{6,4},{8,10},{10,8},{12,14},{14,12},{16,18},{18,... | collective-permute-start | bytes 995336 | tf_op jit(solution)/shard_map/ppermute | solution.py:679
  3.6 2.6 %collective-permute-start = (f32[16,8,128]{2,1,0:T(8,128)S(1)}, f32[16,8,128]{2,1,0:T(8,128)S(1)}, u32[]{:S(2)}, u32[]{:S(2)}) collective-permute-start(f32[16,8,128]{2,1,0:T(8,128)S(1)} %get-tuple-element.17), channel_id=1, source_target_pairs={{0,1},{1,0},{2,3},{3,2},{4,5},{5,4},{6,7},{7,6},{8,9},{9,8},{10,11... | collective-permute-start | bytes 196616 | tf_op jit(solution)/shard_map/ppermute | solution.py:671
  6.2 4.7 %collective-permute-start.1 = (f32[648,128]{1,0:T(8,128)S(1)}, f32[648,128]{1,0:T(8,128)S(1)}, u32[]{:S(2)}, u32[]{:S(2)}) collective-permute-start(f32[648,128]{1,0:T(8,128)S(1)} %far_rows.1.far_ref), channel_id=1, source_target_pairs={{0,30},{2,4},{4,2},{6,8},{8,6},{10,12},{12,10},{14,16},{16,14},{18... | collective-permute-start | bytes 995336 | tf_op jit(solution)/shard_map/ppermute | solution.py:678
  11.0 0.9 %collective-permute-start.2 = (f32[5,8,128]{2,1,0:T(8,128)S(1)}, f32[5,8,128]{2,1,0:T(8,128)S(1)}, u32[]{:S(2)}, u32[]{:S(2)}) collective-permute-start(f32[5,8,128]{2,1,0:T(8,128)S(1)} %get-tuple-element.18), channel_id=1, source_target_pairs={{0,31},{1,30},{2,5},{3,4},{4,3},{5,2},{6,9},{7,8},{8,7},{9,6},{10,... | collective-permute-start | bytes 61448 | tf_op jit(solution)/shard_map/ppermute | solution.py:671
  11.9 5.7 %near_part.1 = (f32[33,128,128]{2,1,0:T(8,128)S(1)}, f32[5,2,144,128]{3,2,1,0:T(8,128)S(1)}, f32[2,2,64,128]{3,2,1,0:T(8,128)S(1)}) custom-call(f32[16,128,128]{2,1,0:T(8,128)S(1)} %get-tuple-element.19.turned_ref, f32[16,128]{1,0:T(8,128)S(1)} %get-tuple-element.16.mask_ref, f32[16,8,128]{2,1,0:T(8,128)S(1)} %collective-permute-done.left_ref.right_ref, ...), custom_call_target="tpu_custom_call" | custom-call | flops 4000000000 | bytes 8000000 | tf_op jit(solution)/shard_map/near_part/pallas_call | solution.py:374
  17.6 0.2 collective-permute-done.2.far_left_ref.far_right_ref
  17.8 2.3 %far_part.1 = (f32[15,128,128]{2,1,0:T(8,128)S(1)}, f32[2,2,64,128]{3,2,1,0:T(8,128)S(1)}) custom-call(f32[16,128]{1,0:T(8,128)S(1)} %get-tuple-element.16.mask_ref, f32[16,8,128]{2,1,0:T(8,128)S(1)} %collective-permute-done.left_ref.right_ref, f32[16,8,128]{2,1,0:T(8,128)S(1)} %collective-permute-done.left_ref.right_ref, ...), custom_call_target="tpu_custom_call" | custom-call | tf_op jit(solution)/shard_map/far_part/pallas_call | solution.py:391
  20.2 1.2 %collective-permute-done.5 = f32[2,64,128]{2,1,0:T(8,128)S(1)} collective-permute-done((f32[2,64,128]{2,1,0:T(8,128)S(1)}, f32[2,64,128]{2,1,0:T(8,128)S(1)}, u32[]{:S(2)}, u32[]{:S(2)}) %collective-permute-start.5) | collective-permute-done | bytes 65568 | tf_op jit(solution)/shard_map/ppermute | solution.py:632
  21.4 1.7 %collective-permute-start.8 = (f32[2,64,128]{2,1,0:T(8,128)S(1)}, f32[2,64,128]{2,1,0:T(8,128)S(1)}, u32[]{:S(2)}, u32[]{:S(2)}) collective-permute-start(f32[2,64,128]{2,1,0:T(8,128)S(1)} %pad_maximum_fusion), channel_id=1, source_target_pairs={{0,5},{1,4},{2,7},{3,6},{4,1},{5,0},{6,3},{7,2},{8,13},{9,12},{10,... | collective-permute-start | bytes 196616 | tf_op jit(solution)/shard_map/ppermute | solution.py:632
  23.2 1.3 %collective-permute-start.7 = (f32[2,64,128]{2,1,0:T(8,128)S(1)}, f32[2,64,128]{2,1,0:T(8,128)S(1)}, u32[]{:S(2)}, u32[]{:S(2)}) collective-permute-start(f32[2,64,128]{2,1,0:T(8,128)S(1)} %pad_maximum_fusion), channel_id=1, source_target_pairs={{0,4},{1,5},{2,6},{3,7},{4,0},{5,1},{6,2},{7,3},{8,12},{9,13},{10,... | collective-permute-start | bytes 196616 | tf_op jit(solution)/shard_map/ppermute | solution.py:632
  24.5 0.5 %collective-permute-start.6 = (f32[2,64,128]{2,1,0:T(8,128)S(1)}, f32[2,64,128]{2,1,0:T(8,128)S(1)}, u32[]{:S(2)}, u32[]{:S(2)}) collective-permute-start(f32[2,64,128]{2,1,0:T(8,128)S(1)} %pad_maximum_fusion), channel_id=1, source_target_pairs={{0,1},{1,0},{2,3},{3,2},{4,5},{5,4},{6,7},{7,6},{8,9},{9,8},{10,11... | collective-permute-start | bytes 196616 | tf_op jit(solution)/shard_map/ppermute | solution.py:632
  25.0 1.7 %collective-permute-done.8 = f32[2,64,128]{2,1,0:T(8,128)S(1)} collective-permute-done((f32[2,64,128]{2,1,0:T(8,128)S(1)}, f32[2,64,128]{2,1,0:T(8,128)S(1)}, u32[]{:S(2)}, u32[]{:S(2)}) %collective-permute-start.8) | collective-permute-done | bytes 65568 | tf_op jit(solution)/shard_map/ppermute | solution.py:632
  26.7 1.2 %collective-permute-done.7 = f32[2,64,128]{2,1,0:T(8,128)S(1)} collective-permute-done((f32[2,64,128]{2,1,0:T(8,128)S(1)}, f32[2,64,128]{2,1,0:T(8,128)S(1)}, u32[]{:S(2)}, u32[]{:S(2)}) %collective-permute-start.7) | collective-permute-done | bytes 65568 | tf_op jit(solution)/shard_map/ppermute | solution.py:632
  28.0 0.8 %collective-permute-done.6 = f32[2,64,128]{2,1,0:T(8,128)S(1)} collective-permute-done((f32[2,64,128]{2,1,0:T(8,128)S(1)}, f32[2,64,128]{2,1,0:T(8,128)S(1)}, u32[]{:S(2)}, u32[]{:S(2)}) %collective-permute-start.6) | collective-permute-done | bytes 65568 | tf_op jit(solution)/shard_map/ppermute | solution.py:632
  28.8 2.9 %collective-permute-start.11 = (f32[2,64,128]{2,1,0:T(8,128)S(1)}, f32[2,64,128]{2,1,0:T(8,128)S(1)}, u32[]{:S(2)}, u32[]{:S(2)}) collective-permute-start(f32[2,64,128]{2,1,0:T(8,128)S(1)} %pad_maximum_fusion.1), channel_id=1, source_target_pairs={{0,24},{1,25},{2,26},{3,27},{4,28},{5,29},{6,30},{7,31},{8,16},{9,... | collective-permute-start | bytes 196616 | tf_op jit(solution)/shard_map/ppermute | solution.py:632
  31.7 1.5 %collective-permute-start.9 = (f32[2,64,128]{2,1,0:T(8,128)S(1)}, f32[2,64,128]{2,1,0:T(8,128)S(1)}, u32[]{:S(2)}, u32[]{:S(2)}) collective-permute-start(f32[2,64,128]{2,1,0:T(8,128)S(1)} %pad_maximum_fusion.1), channel_id=1, source_target_pairs={{0,8},{1,9},{2,10},{3,11},{4,12},{5,13},{6,14},{7,15},{8,0},{9,1},... | collective-permute-start | bytes 196616 | tf_op jit(solution)/shard_map/ppermute | solution.py:632
  33.2 1.7 %collective-permute-done.11 = f32[2,64,128]{2,1,0:T(8,128)S(1)} collective-permute-done((f32[2,64,128]{2,1,0:T(8,128)S(1)}, f32[2,64,128]{2,1,0:T(8,128)S(1)}, u32[]{:S(2)}, u32[]{:S(2)}) %collective-permute-start.11) | collective-permute-done | bytes 65568 | tf_op jit(solution)/shard_map/ppermute | solution.py:632
  34.9 2.4 %collective-permute-done.10 = f32[2,64,128]{2,1,0:T(8,128)S(1)} collective-permute-done((f32[2,64,128]{2,1,0:T(8,128)S(1)}, f32[2,64,128]{2,1,0:T(8,128)S(1)}, u32[]{:S(2)}, u32[]{:S(2)}) %collective-permute-start.10) | collective-permute-done | bytes 65568 | tf_op jit(solution)/shard_map/ppermute | solution.py:632
  37.5 0.6 %split.1 = (bf16[48,128,128]{2,1,0:T(8,128)(2,1)S(1)}, bf16[48,128,128]{2,1,0:T(8,128)(2,1)S(1)}, bf16[48,128,128]{2,1,0:T(8,128)(2,1)S(1)}) custom-call(f32[33,128,128]{2,1,0:T(8,128)S(1)} %get-tuple-element.25.near_ref, f32[15,128,128]{2,1,0:T(8,128)S(1)} %get-tuple-element.26.far_ref), custom_call_target="tpu_custom_call" | custom-call | flops 10000000 | bytes 2000000 | tf_op jit(solution)/shard_map/split/pallas_call | solution.py:487
  38.0 0.7 %collective-permute-done.12 = f32[2,64,128]{2,1,0:T(8,128)S(1)} collective-permute-done((f32[2,64,128]{2,1,0:T(8,128)S(1)}, f32[2,64,128]{2,1,0:T(8,128)S(1)}, u32[]{:S(2)}, u32[]{:S(2)}) %collective-permute-start.12) | collective-permute-done | bytes 65568 | tf_op jit(solution)/shard_map/ppermute | solution.py:632
  38.7 8.6 %orthonormal.1 = (f32[128,3,16,128]{3,2,1,0:T(8,128)}, f32[128,128]{1,0:T(8,128)}) custom-call(f32[2,2,64,128]{3,2,1,0:T(8,128)S(1)} %maximum_select_fusion.gram_ref, bf16[48,128,128]{2,1,0:T(8,128)(2,1)S(1)} %get-tuple-element.27.first_ref, bf16[48,128,128]{2,1,0:T(8,128)(2,1)S(1)} %get-tuple-element.28.second_ref, ...), custom_call_target="tpu_custom_call" | custom-call | tf_op jit(solution)/shard_map/orthonormal/pallas_call | solution.py:611
  (19 shorter events, 0.5 us)
Async XLA Ops:
  1.3 1.2 %copy-start = (f32[128,16,128]{2,1,0:T(8,128)S(1)}, f32[128,16,128]{2,1,0:T(8,128)}, u32[]{:S(2)}) copy-start(f32[128,16,128]{2,1,0:T(8,128)} %param.2) | copy-start | bytes 3145732
  3.1 8.8 %collective-permute-start.3 = (f32[648,128]{1,0:T(8,128)S(1)}, f32[648,128]{1,0:T(8,128)S(1)}, u32[]{:S(2)}, u32[]{:S(2)}) collective-permute-start(f32[648,128]{1,0:T(8,128)S(1)} %get-tuple-element.20), channel_id=1, source_target_pairs={{0,2},{2,0},{4,6},{6,4},{8,10},{10,8},{12,14},{14,12},{16,18},{18,... | collective-permute-start | bytes 995336 | tf_op jit(solution)/shard_map/ppermute | solution.py:679
  3.6 8.3 %collective-permute-start = (f32[16,8,128]{2,1,0:T(8,128)S(1)}, f32[16,8,128]{2,1,0:T(8,128)S(1)}, u32[]{:S(2)}, u32[]{:S(2)}) collective-permute-start(f32[16,8,128]{2,1,0:T(8,128)S(1)} %get-tuple-element.17), channel_id=1, source_target_pairs={{0,1},{1,0},{2,3},{3,2},{4,5},{5,4},{6,7},{7,6},{8,9},{9,8},{10,11... | collective-permute-start | bytes 196616 | tf_op jit(solution)/shard_map/ppermute | solution.py:671
  6.1 5.7 %collective-permute-start.4 = (f32[5,8,128]{2,1,0:T(8,128)S(1)}, f32[5,8,128]{2,1,0:T(8,128)S(1)}, u32[]{:S(2)}, u32[]{:S(2)}) collective-permute-start(f32[5,8,128]{2,1,0:T(8,128)S(1)} %get-tuple-element.21), channel_id=1, source_target_pairs={{0,3},{1,2},{2,1},{3,0},{4,7},{5,6},{6,5},{7,4},{8,11},{9,10},{10,... | collective-permute-start | bytes 61448 | tf_op jit(solution)/shard_map/ppermute | solution.py:671
  6.2 11.6 %collective-permute-start.1 = (f32[648,128]{1,0:T(8,128)S(1)}, f32[648,128]{1,0:T(8,128)S(1)}, u32[]{:S(2)}, u32[]{:S(2)}) collective-permute-start(f32[648,128]{1,0:T(8,128)S(1)} %far_rows.1.far_ref), channel_id=1, source_target_pairs={{0,30},{2,4},{4,2},{6,8},{8,6},{10,12},{12,10},{14,16},{16,14},{18... | collective-permute-start | bytes 995336 | tf_op jit(solution)/shard_map/ppermute | solution.py:678
  11.0 6.8 %collective-permute-start.2 = (f32[5,8,128]{2,1,0:T(8,128)S(1)}, f32[5,8,128]{2,1,0:T(8,128)S(1)}, u32[]{:S(2)}, u32[]{:S(2)}) collective-permute-start(f32[5,8,128]{2,1,0:T(8,128)S(1)} %get-tuple-element.18), channel_id=1, source_target_pairs={{0,31},{1,30},{2,5},{3,4},{4,3},{5,2},{6,9},{7,8},{8,7},{9,6},{10,... | collective-permute-start | bytes 61448 | tf_op jit(solution)/shard_map/ppermute | solution.py:671
  20.1 1.3 %collective-permute-start.5 = (f32[2,64,128]{2,1,0:T(8,128)S(1)}, f32[2,64,128]{2,1,0:T(8,128)S(1)}, u32[]{:S(2)}, u32[]{:S(2)}) collective-permute-start(f32[2,64,128]{2,1,0:T(8,128)S(1)} %get-tuple-element.37), channel_id=1, source_target_pairs={{0,2},{1,3},{2,0},{3,1},{4,6},{5,7},{6,4},{7,5},{8,10},{9,11},{10,... | collective-permute-start | bytes 196616 | tf_op jit(solution)/shard_map/ppermute | solution.py:632
  21.4 5.3 %collective-permute-start.8 = (f32[2,64,128]{2,1,0:T(8,128)S(1)}, f32[2,64,128]{2,1,0:T(8,128)S(1)}, u32[]{:S(2)}, u32[]{:S(2)}) collective-permute-start(f32[2,64,128]{2,1,0:T(8,128)S(1)} %pad_maximum_fusion), channel_id=1, source_target_pairs={{0,5},{1,4},{2,7},{3,6},{4,1},{5,0},{6,3},{7,2},{8,13},{9,12},{10,... | collective-permute-start | bytes 196616 | tf_op jit(solution)/shard_map/ppermute | solution.py:632
  23.2 4.8 %collective-permute-start.7 = (f32[2,64,128]{2,1,0:T(8,128)S(1)}, f32[2,64,128]{2,1,0:T(8,128)S(1)}, u32[]{:S(2)}, u32[]{:S(2)}) collective-permute-start(f32[2,64,128]{2,1,0:T(8,128)S(1)} %pad_maximum_fusion), channel_id=1, source_target_pairs={{0,4},{1,5},{2,6},{3,7},{4,0},{5,1},{6,2},{7,3},{8,12},{9,13},{10,... | collective-permute-start | bytes 196616 | tf_op jit(solution)/shard_map/ppermute | solution.py:632
  24.5 4.3 %collective-permute-start.6 = (f32[2,64,128]{2,1,0:T(8,128)S(1)}, f32[2,64,128]{2,1,0:T(8,128)S(1)}, u32[]{:S(2)}, u32[]{:S(2)}) collective-permute-start(f32[2,64,128]{2,1,0:T(8,128)S(1)} %pad_maximum_fusion), channel_id=1, source_target_pairs={{0,1},{1,0},{2,3},{3,2},{4,5},{5,4},{6,7},{7,6},{8,9},{9,8},{10,11... | collective-permute-start | bytes 196616 | tf_op jit(solution)/shard_map/ppermute | solution.py:632
  28.8 6.1 %collective-permute-start.11 = (f32[2,64,128]{2,1,0:T(8,128)S(1)}, f32[2,64,128]{2,1,0:T(8,128)S(1)}, u32[]{:S(2)}, u32[]{:S(2)}) collective-permute-start(f32[2,64,128]{2,1,0:T(8,128)S(1)} %pad_maximum_fusion.1), channel_id=1, source_target_pairs={{0,24},{1,25},{2,26},{3,27},{4,28},{5,29},{6,30},{7,31},{8,16},{9,... | collective-permute-start | bytes 196616 | tf_op jit(solution)/shard_map/ppermute | solution.py:632
  31.7 5.6 %collective-permute-start.10 = (f32[2,64,128]{2,1,0:T(8,128)S(1)}, f32[2,64,128]{2,1,0:T(8,128)S(1)}, u32[]{:S(2)}, u32[]{:S(2)}) collective-permute-start(f32[2,64,128]{2,1,0:T(8,128)S(1)} %pad_maximum_fusion.1), channel_id=1, source_target_pairs={{0,16},{1,17},{2,18},{3,19},{4,20},{5,21},{6,22},{7,23},{8,24},{9,... | collective-permute-start | bytes 196616 | tf_op jit(solution)/shard_map/ppermute | solution.py:632
  31.7 5.6 %collective-permute-start.9 = (f32[2,64,128]{2,1,0:T(8,128)S(1)}, f32[2,64,128]{2,1,0:T(8,128)S(1)}, u32[]{:S(2)}, u32[]{:S(2)}) collective-permute-start(f32[2,64,128]{2,1,0:T(8,128)S(1)} %pad_maximum_fusion.1), channel_id=1, source_target_pairs={{0,8},{1,9},{2,10},{3,11},{4,12},{5,13},{6,14},{7,15},{8,0},{9,1},... | collective-permute-start | bytes 196616 | tf_op jit(solution)/shard_map/ppermute | solution.py:632
  37.4 1.3 %collective-permute-start.12 = (f32[2,64,128]{2,1,0:T(8,128)S(1)}, f32[2,64,128]{2,1,0:T(8,128)S(1)}, u32[]{:S(2)}, u32[]{:S(2)}) collective-permute-start(f32[2,64,128]{2,1,0:T(8,128)S(1)} %get-tuple-element.39), channel_id=1, source_target_pairs={{0,2},{1,3},{2,0},{3,1},{4,6},{5,7},{6,4},{7,5},{8,10},{9,11},{10,... | collective-permute-start | bytes 196616 | tf_op jit(solution)/shard_map/ppermute | solution.py:632
